TPU v7x, 32 devices: a whole 2x2x4 slice. The times are simulated.
32 devices in a mesh: groups: 2 (over y), leaf: 4 (over z), sub: 2 (over x), chan: 2 (over core).
Axes of the slice: x: 2, y: 2, z: 4, core: 2. Of those that a mesh axis runs over, the one named last changes fastest.
Arguments:
- charges: bfloat16 [2, 8, 32768], P('chan', None, ('groups', 'leaf', 'sub')), parts along dimension 2, may hold values from -6 to 6
- positions: float32 [3, 32768], P(None, ('groups', 'leaf', 'sub')), parts along dimension 1, may hold values from -6 to 6
- harmonics: bfloat16 [49, 32768], P(None, ('groups', 'leaf', 'sub')), parts along dimension 1, may hold values from -1.5 to 1.5
- operators: bfloat16 [316, 49, 49], replicated, may hold values from -0.0625 to 0.0625
- leaf_atoms: int32 [16, 64], P(('groups', 'leaf', 'sub')), parts along dimension 0, may hold values from 1 to 32, 1024 in all within a row
- near_lists: int32 [27, 1024], P(None, ('groups', 'leaf', 'sub')), parts along dimension 1, may hold values from 0 to 96, as said below
- requests: int32 [16, 8, 8], P(('groups', 'leaf', 'sub')), parts along dimension 0, may hold values from 0 to 63, as said below
- m2l_slots: int32 [316, 1024], P(None, ('groups', 'leaf', 'sub')), parts along dimension 1, may hold values from 0 to 128, as said below
Outputs:
- potentials: float32 [2, 8, 32768], P('chan', None, ('groups', 'leaf', 'sub')), parts along dimension 2
There are 2 independent parts, one for each index of `groups`. A program takes and returns all parts, laid end to end along the dimension named above; an argument that names none is the same for every part. Nothing has to cross between parts.
Inputs may be any that keep to these rules, and one draw needn't show every extreme that they name: `leaf_atoms`: each device's 64 counts sum to 1024. `near_lists`: entries name distinct values within one leaf's list; 96 means none. `requests`: A device reads no leaves from itself; unused entries are 0. `m2l_slots`: 128 means none; slots of a device's own rank among the received blocks, and unused request entries, are never named.
All inputs are finite; a program needn't handle non-finite values.
Results may differ from a plain program's by a relative error of at most 0.0037.
Values may be sent and summed in bfloat16 or wider, within the bound.
A program may use at most 64 MiB of HBM per device.

v0:
```python
import math

import jax
import jax.numpy as jnp
from jax import lax
from jax.sharding import PartitionSpec as P

HALO = 16


SOFT_SQ = 0.0625
NEAR_GAIN = 0.1


def padded(block, sides, width):
    for axis, dim in sides:
        count = lax.axis_size(axis)
        forward = [(i, i + 1) for i in range(count - 1)]
        backward = [(target, source) for source, target in forward]
        low = lax.ppermute(
            lax.slice_in_dim(block, block.shape[dim] - width, None, axis=dim), axis, forward
        )
        high = lax.ppermute(lax.slice_in_dim(block, 0, width, axis=dim), axis, backward)
        block = jnp.concatenate([low, block, high], axis=dim)
    return block


def near_tile(block_parts):
    targets, nbr_pos, nbr_charge = block_parts
    squared = sum(
        (
            (targets[coordinate][None, :, :, None] - nbr_pos[coordinate][:, :, None, :]) ** 2
            for coordinate in range(3)
        )
    )
    kernel = lax.rsqrt(squared + SOFT_SQ).astype(jnp.bfloat16)
    return jnp.einsum("nlij,cnlj->cli", kernel, nbr_charge, preferred_element_type=jnp.float32)


def per_device(
    charges, positions, harmonics, operators, leaf_atoms, near_lists, requests, m2l_slots
):
    leaf_count = leaf_atoms.shape[1]
    atom_slots = positions.shape[1] // leaf_count
    term_count = harmonics.shape[0]
    channel_count = charges.shape[1]
    width = term_count * channel_count
    alive_mask = (jnp.arange(atom_slots)[None, :] < leaf_atoms[0][:, None]).reshape(-1)
    masked = charges[0] * alive_mask.astype(jnp.bfloat16)[None, :]
    harmonic_grid = harmonics.reshape(term_count, leaf_count, atom_slots)
    charge_grid = masked.reshape(channel_count, leaf_count, atom_slots)
    moments = (
        jnp.einsum("tla,cla->ltc", harmonic_grid, charge_grid, preferred_element_type=jnp.float32)
        .astype(jnp.bfloat16)
        .reshape(leaf_count, width)
    )
    wanted = requests[0]
    asked_for = lax.all_to_all(wanted, ("leaf", "sub"), split_axis=0, concat_axis=0, tiled=True)
    fetched = lax.all_to_all(
        moments[asked_for], ("leaf", "sub"), split_axis=0, concat_axis=0, tiled=True
    )
    fetched = fetched.reshape(-1, width)
    combined = jnp.concatenate([moments, fetched, jnp.zeros((1, width), jnp.bfloat16)], axis=0)
    type_count = operators.shape[0]
    slot_blocks = m2l_slots.reshape(4, type_count // 4, leaf_count)
    op_blocks = operators.reshape(4, type_count // 4, term_count, term_count)

    def accumulate(running, block_pair):
        slot_table, op_table = block_pair
        sources = combined[slot_table].reshape(
            slot_table.shape[0], leaf_count, term_count, channel_count
        )
        return (
            running
            + jnp.einsum("kuv,klvc->luc", op_table, sources, preferred_element_type=jnp.float32),
            None,
        )

    start = jnp.zeros((leaf_count, term_count, channel_count), jnp.float32)
    local_exp = lax.scan(accumulate, start, (slot_blocks, op_blocks))[0].astype(jnp.bfloat16)
    far_field = jnp.einsum(
        "tla,ltc->cla", harmonic_grid, local_exp, preferred_element_type=jnp.float32
    )
    stacked = jnp.concatenate([positions, masked.astype(jnp.float32)], axis=0)
    extended = padded(stacked, ((("leaf", "sub"), 1),), HALO * atom_slots)
    extended = jnp.concatenate(
        [extended, jnp.zeros((stacked.shape[0], atom_slots), jnp.float32)], axis=1
    )
    extended = extended.reshape(stacked.shape[0], -1, atom_slots)
    nbr_pos = extended[:3][:, near_lists]
    nbr_charge = extended[3:].astype(jnp.bfloat16)[:, near_lists]
    block_size = math.gcd(leaf_count, 32)
    group_count = leaf_count // block_size
    neighbours = near_lists.shape[0]
    target_blocks = positions.reshape(3, group_count, block_size, atom_slots).transpose(1, 0, 2, 3)
    pos_blocks = nbr_pos.reshape(3, neighbours, group_count, block_size, atom_slots).transpose(
        2, 0, 1, 3, 4
    )
    charge_blocks = nbr_charge.reshape(
        channel_count, neighbours, group_count, block_size, atom_slots
    ).transpose(2, 0, 1, 3, 4)
    near_parts = lax.map(near_tile, (target_blocks, pos_blocks, charge_blocks))
    near_field = NEAR_GAIN * near_parts.transpose(1, 0, 2, 3).reshape(
        channel_count, leaf_count, atom_slots
    )
    total = (far_field + near_field) * alive_mask.astype(jnp.float32).reshape(
        1, leaf_count, atom_slots
    )
    return total.reshape(1, channel_count, leaf_count * atom_slots)


def solution(mesh):
    return jax.shard_map(
        per_device,
        mesh=mesh,
        in_specs=(
            P("chan", None, ("groups", "leaf", "sub")),
            P(None, ("groups", "leaf", "sub")),
            P(None, ("groups", "leaf", "sub")),
            P(),
            P(("groups", "leaf", "sub"), None),
            P(None, ("groups", "leaf", "sub")),
            P(("groups", "leaf", "sub"), None, None),
            P(None, ("groups", "leaf", "sub")),
        ),
        out_specs=P("chan", None, ("groups", "leaf", "sub")),
        check_vma=False,
    )
```

profile of v0, /device:TPU:0, one launch (start us, length us, event | category | flops | bytes accessed | tf_op | source)
XLA Modules:
  0.0 283.0 jit_solution(8944596576130309125)
XLA Ops:
  0.0 1.3 fusion.20
  1.4 0.8 fusion.19
  2.9 4.8 %collective-permute-start = (f32[11,512]{1,0:T(8,128)S(1)}, f32[11,512]{1,0:T(8,128)S(1)}, u32[]{:S(2)}, u32[]{:S(2)}) collective-permute-start(f32[11,512]{1,0:T(8,128)S(1)} %get-tuple-element.135), channel_id=1, source_target_pairs={{0,2},{2,4},{4,6},{6,8},{8,10},{10,12},{12,14},{1,3},{3,5},{5,7},{... | collective-permute-start | bytes 67592 | tf_op jit(solution)/shard_map/ppermute | solution.py:20
  7.8 1.3 collective-permute-start.1
  9.1 7.0 %all-to-all-start = ((s32[8,1,8]{2,1,0:T(1,128)}), s32[8,1,8]{2,1,0:T(1,128)S(1)}, u32[]{:S(2)}, u32[]{:S(2)}) async-start(s32[8,1,8]{2,1,0:T(1,128)} %bitcast.132), calls=%async_computation | async-start | bytes 8192 | tf_op jit(solution)/shard_map/all_to_all | solution.py:58
  16.0 1.5 reshape.164
  17.6 0.9 squeeze.28
  19.3 1.2 copy.56
  21.8 4.9 %reshape.162 = bf16[4,79,49,49]{1,0,3,2:T(4,128)(2,1)S(1)} reshape(bf16[316,49,49]{0,2,1:T(8,128)(2,1)} %param.15) | data formatting | bytes 3034864 | tf_op jit(solution)/shard_map/reshape | solution.py:66
  26.7 1.9 copy.64
  28.6 0.8 reshape.158
  29.5 1.3 gather_fusion.1
  30.8 6.0 %all-to-all-start.1 = ((bf16[8,8,392]{2,1,0:T(8,128)(2,1)}), bf16[8,8,392]{2,1,0:T(8,128)(2,1)}, u32[]{:S(2)}, u32[]{:S(2)}) async-start(bf16[8,8,392]{2,1,0:T(8,128)(2,1)} %bitcast.18), calls=%async_computation.1 | async-start | bytes 131072 | tf_op jit(solution)/shard_map/all_to_all | solution.py:59
  37.8 5.7 %gather_fusion.2 = bf16[1728,8,32]{2,1,0:T(8,128)(2,1)} fusion(bf16[8,97,32]{2,0,1:T(8,128)(2,1)S(1)} %copy.66, s32[2048]{0:T(1024)S(1)} %pad_clamp_fusion.1), kind=kCustom, calls=%fused_computation.2 | custom fusion | bytes 1776384 | tf_op jit(solution)/shard_map/gather | solution.py:91
  43.5 9.4 %copy.80 = bf16[8,27,2,32,32]{3,2,4,1,0:T(2,128)(2,1)S(1)} copy(bf16[8,27,2,32,32]{4,0,3,2,1:T(8,128)(2,1)} %bitcast.118) | data formatting | bytes 1769472 | tf_op jit(solution)/shard_map/reshape | solution.py:99
  52.9 7.5 %copy.71 = bf16[2,8,27,32,32]{4,1,2,3,0:T(8,128)(2,1)} copy(bf16[2,8,27,32,32]{3,0,4,2,1:T(2,128)(2,1)S(1)} %bitcast.119) | data formatting | bytes 1769472 | tf_op jit(solution)/shard_map/while | solution.py:102
  60.4 0.9 slice.45
  61.4 6.2 %gather_fusion.3 = f32[1728,3,32]{2,1,0:T(4,128)} fusion(f32[3,97,32]{2,0,1:T(4,128)S(1)} %copy.69, s32[2048]{0:T(1024)S(1)} %pad_clamp_fusion.1), kind=kCustom, calls=%fused_computation.3 | custom fusion | bytes 1334016 | tf_op jit(solution)/shard_map/gather | solution.py:90
  67.6 3.2 %copy.70 = f32[27,64,3,32]{1,3,0,2:T(8,128)S(1)} copy(f32[27,64,3,32]{3,2,1,0:T(4,128)} %bitcast.123) | data formatting | bytes 1327104 | tf_op jit(solution)/shard_map/gather | solution.py:90
  70.8 3.0 %reshape.165 = f32[3,27,2,32,32]{3,2,4,1,0:T(2,128)} reshape(f32[3,27,64,32]{2,3,1,0:T(8,128)S(1)} %bitcast.124) | data formatting | bytes 1327104 | tf_op jit(solution)/shard_map/reshape | solution.py:96
  73.8 24.1 %while.21 = (s32[]{:T(128)}, f32[2,8,32,32]{3,1,2,0:T(8,128)S(1)}, bf16[2,8,27,32,32]{4,1,2,3,0:T(8,128)(2,1)}, f32[2,3,32,32]{3,2,0,1:T(8,128)S(1)}, f32[2,3,27...) while((s32[]{:T(128)}, f32[2,8,32,32]{3,1,2,0:T(8,128)S(1)}, ...), condition=%wide.region_3.4_spmd, body=%wide.region_2.3_spmd.sunk | while | flops 23003140 | bytes 4899973 | solution.py:102
  73.8 3.2 %constant_dynamic-slice_fusion.6 = (f32[1,1,27,32,32]{3,0,4,2,1:T(1,128)S(1)}, f32[1,1,27,32,32]{3,0,4,2,1:T(1,128)S(1)}, f32[1,1,27,32,32]{3,0,4,2,1:T(1,128)S(1)}) fusion(f32[2,3,27,32,32]{3,0,4,2,1:T(2,128)} %get-tuple-element.235, s32[]{:T(128)} %get-tuple-element.222, s32[]{:T(128)S(6)} %add.96, s32[]{:T(128)S(6)} %add.97), kind=kLoop, calls=%fused_computation.15.clone.1 | loop fusion | bytes 663564 | tf_op jit(solution)/shard_map/while/body/eval_jaxpr/slice | solution.py:32
  79.2 6.7 %fusion.32 = f32[2,8,32,32]{3,1,2,0:T(8,128)S(1)} fusion(f32[2,8,32,32]{3,1,2,0:T(8,128)S(1)} %get-tuple-element.223, s32[]{:T(128)} %get-tuple-element.222, f32[27,32,32]{2,0,1:T(8,128)S(1)} %bitcast.120, f32[32,32]{1,0:T(8,128)S(1)} %get-tuple-element.203, f32[27,32,32]{2,0,1:T(8,128)S(1)} %bitcast.121, f32[32,32]{1,0:T(8,128)S(1)} %get-tuple-element.205, ...), kind=kOutput, calls=%fused_computation.9.clone.1 | convolution fusion | flops 23003136 | bytes 3523584 | tf_op jit(solution)/shard_map/while/body/eval_jaxpr/nlij,cnlj->cli/dot_general | solution.py:37
  85.9 3.1 %constant_dynamic-slice_fusion.6 = (f32[1,1,27,32,32]{3,0,4,2,1:T(1,128)S(1)}, f32[1,1,27,32,32]{3,0,4,2,1:T(1,128)S(1)}, f32[1,1,27,32,32]{3,0,4,2,1:T(1,128)S(1)}) fusion(f32[2,3,27,32,32]{3,0,4,2,1:T(2,128)} %get-tuple-element.235, s32[]{:T(128)} %get-tuple-element.222, s32[]{:T(128)S(6)} %add.96, s32[]{:T(128)S(6)} %add.97), kind=kLoop, calls=%fused_computation.15.clone.1 | loop fusion | bytes 663564 | tf_op jit(solution)/shard_map/while/body/eval_jaxpr/slice | solution.py:32
  91.2 6.7 %fusion.32 = f32[2,8,32,32]{3,1,2,0:T(8,128)S(1)} fusion(f32[2,8,32,32]{3,1,2,0:T(8,128)S(1)} %get-tuple-element.223, s32[]{:T(128)} %get-tuple-element.222, f32[27,32,32]{2,0,1:T(8,128)S(1)} %bitcast.120, f32[32,32]{1,0:T(8,128)S(1)} %get-tuple-element.203, f32[27,32,32]{2,0,1:T(8,128)S(1)} %bitcast.121, f32[32,32]{1,0:T(8,128)S(1)} %get-tuple-element.205, ...), kind=kOutput, calls=%fused_computation.9.clone.1 | convolution fusion | flops 23003136 | bytes 3523584 | tf_op jit(solution)/shard_map/while/body/eval_jaxpr/nlij,cnlj->cli/dot_general | solution.py:37
  97.9 1.0 copy.61
  99.2 182.4 %while.22 = (s32[]{:T(128)}, f32[64,49,8]{0,1,2:T(8,128)S(1)}, s32[4,79,64]{1,0,2:T(4,128)}, bf16[129,392]{1,0:T(8,128)(2,1)S(1)}, bf16[4,79,49,49]{1,2,3,0:T(8,128)(2,1)}, /*index=5*/s32[]{:T(128)}, s32[]{:T(128)}) while((s32[]{:T(128)}, f32[64,49,8]{0,1,2:T(8,128)S(1)}, s32[4,79,64]{1,0,2:T(4,128)}, ...), condition=%wide.region_1.2_spmd.clone, body=%wide.region_0.1_spmd.clone.sunk | while | flops 194301760 | bytes 32938072 | solution.py:80
  99.2 1.0 constant_dynamic-slice_fusion.7
  100.4 21.3 %gather_fusion = bf16[5056,392]{1,0:T(8,128)(2,1)} fusion(bf16[129,392]{1,0:T(8,128)(2,1)S(1)} %get-tuple-element.257, s32[5120]{0:T(1024)S(1)} %pad_clamp_fusion.4), kind=kCustom, calls=%fused_computation.clone.clone.1 | custom fusion | bytes 7948032 | tf_op jit(solution)/shard_map/while/body/eval_jaxpr/gather | solution.py:70
  121.7 7.2 %copy.98 = bf16[5056,392]{0,1:T(8,128)(2,1)} copy(bf16[5056,392]{1,0:T(8,128)(2,1)} %gather_fusion) | data formatting | bytes 7927808 | tf_op jit(solution)/shard_map/while/body/eval_jaxpr/gather | solution.py:70
  128.9 10.9 %reshape.222 = bf16[79,64,49,8]{1,0,3,2:T(8,128)(2,1)} reshape(bf16[5056,392]{0,1:T(8,128)(2,1)} %copy.98) | data formatting | bytes 7927808 | tf_op jit(solution)/shard_map/while/body/eval_jaxpr/reshape | solution.py:70
  139.8 5.0 %fusion.35 = f32[64,49,8]{0,1,2:T(8,128)S(1)} fusion(bf16[79,64,49,8]{1,0,3,2:T(8,128)(2,1)} %reshape.222, bf16[4,79,49,49]{1,2,3,0:T(8,128)(2,1)} %get-tuple-element.258, s32[]{:T(128)} %get-tuple-element.247, f32[64,49,8]{0,1,2:T(8,128)S(1)} %get-tuple-element.248, pred[]{:T(512)S(6)} %compare.3), kind=kOutput, calls=%fused_computation.20.clone.1 | convolution fusion | flops 194281472 | bytes 8931841 | tf_op jit(solution)/shard_map/while/body/eval_jaxpr/kuv,klvc->luc/dot_general | solution.py:75
  144.8 0.9 constant_dynamic-slice_fusion.7
  146.0 21.3 %gather_fusion = bf16[5056,392]{1,0:T(8,128)(2,1)} fusion(bf16[129,392]{1,0:T(8,128)(2,1)S(1)} %get-tuple-element.257, s32[5120]{0:T(1024)S(1)} %pad_clamp_fusion.4), kind=kCustom, calls=%fused_computation.clone.clone.1 | custom fusion | bytes 7948032 | tf_op jit(solution)/shard_map/while/body/eval_jaxpr/gather | solution.py:70
  167.3 7.2 %copy.98 = bf16[5056,392]{0,1:T(8,128)(2,1)} copy(bf16[5056,392]{1,0:T(8,128)(2,1)} %gather_fusion) | data formatting | bytes 7927808 | tf_op jit(solution)/shard_map/while/body/eval_jaxpr/gather | solution.py:70
  174.5 10.9 %reshape.222 = bf16[79,64,49,8]{1,0,3,2:T(8,128)(2,1)} reshape(bf16[5056,392]{0,1:T(8,128)(2,1)} %copy.98) | data formatting | bytes 7927808 | tf_op jit(solution)/shard_map/while/body/eval_jaxpr/reshape | solution.py:70
  185.4 5.0 %fusion.35 = f32[64,49,8]{0,1,2:T(8,128)S(1)} fusion(bf16[79,64,49,8]{1,0,3,2:T(8,128)(2,1)} %reshape.222, bf16[4,79,49,49]{1,2,3,0:T(8,128)(2,1)} %get-tuple-element.258, s32[]{:T(128)} %get-tuple-element.247, f32[64,49,8]{0,1,2:T(8,128)S(1)} %get-tuple-element.248, pred[]{:T(512)S(6)} %compare.3), kind=kOutput, calls=%fused_computation.20.clone.1 | convolution fusion | flops 194281472 | bytes 8931841 | tf_op jit(solution)/shard_map/while/body/eval_jaxpr/kuv,klvc->luc/dot_general | solution.py:75
  190.4 0.9 constant_dynamic-slice_fusion.7
  191.5 21.3 %gather_fusion = bf16[5056,392]{1,0:T(8,128)(2,1)} fusion(bf16[129,392]{1,0:T(8,128)(2,1)S(1)} %get-tuple-element.257, s32[5120]{0:T(1024)S(1)} %pad_clamp_fusion.4), kind=kCustom, calls=%fused_computation.clone.clone.1 | custom fusion | bytes 7948032 | tf_op jit(solution)/shard_map/while/body/eval_jaxpr/gather | solution.py:70
  212.9 7.2 %copy.98 = bf16[5056,392]{0,1:T(8,128)(2,1)} copy(bf16[5056,392]{1,0:T(8,128)(2,1)} %gather_fusion) | data formatting | bytes 7927808 | tf_op jit(solution)/shard_map/while/body/eval_jaxpr/gather | solution.py:70
  220.1 10.9 %reshape.222 = bf16[79,64,49,8]{1,0,3,2:T(8,128)(2,1)} reshape(bf16[5056,392]{0,1:T(8,128)(2,1)} %copy.98) | data formatting | bytes 7927808 | tf_op jit(solution)/shard_map/while/body/eval_jaxpr/reshape | solution.py:70
  231.0 5.0 %fusion.35 = f32[64,49,8]{0,1,2:T(8,128)S(1)} fusion(bf16[79,64,49,8]{1,0,3,2:T(8,128)(2,1)} %reshape.222, bf16[4,79,49,49]{1,2,3,0:T(8,128)(2,1)} %get-tuple-element.258, s32[]{:T(128)} %get-tuple-element.247, f32[64,49,8]{0,1,2:T(8,128)S(1)} %get-tuple-element.248, pred[]{:T(512)S(6)} %compare.3), kind=kOutput, calls=%fused_computation.20.clone.1 | convolution fusion | flops 194281472 | bytes 8931841 | tf_op jit(solution)/shard_map/while/body/eval_jaxpr/kuv,klvc->luc/dot_general | solution.py:75
  236.0 0.9 constant_dynamic-slice_fusion.7
  237.1 21.3 %gather_fusion = bf16[5056,392]{1,0:T(8,128)(2,1)} fusion(bf16[129,392]{1,0:T(8,128)(2,1)S(1)} %get-tuple-element.257, s32[5120]{0:T(1024)S(1)} %pad_clamp_fusion.4), kind=kCustom, calls=%fused_computation.clone.clone.1 | custom fusion | bytes 7948032 | tf_op jit(solution)/shard_map/while/body/eval_jaxpr/gather | solution.py:70
  258.4 7.2 %copy.98 = bf16[5056,392]{0,1:T(8,128)(2,1)} copy(bf16[5056,392]{1,0:T(8,128)(2,1)} %gather_fusion) | data formatting | bytes 7927808 | tf_op jit(solution)/shard_map/while/body/eval_jaxpr/gather | solution.py:70
  265.7 10.9 %reshape.222 = bf16[79,64,49,8]{1,0,3,2:T(8,128)(2,1)} reshape(bf16[5056,392]{0,1:T(8,128)(2,1)} %copy.98) | data formatting | bytes 7927808 | tf_op jit(solution)/shard_map/while/body/eval_jaxpr/reshape | solution.py:70
  276.5 5.0 %fusion.35 = f32[64,49,8]{0,1,2:T(8,128)S(1)} fusion(bf16[79,64,49,8]{1,0,3,2:T(8,128)(2,1)} %reshape.222, bf16[4,79,49,49]{1,2,3,0:T(8,128)(2,1)} %get-tuple-element.258, s32[]{:T(128)} %get-tuple-element.247, f32[64,49,8]{0,1,2:T(8,128)S(1)} %get-tuple-element.248, pred[]{:T(512)S(6)} %compare.3), kind=kOutput, calls=%fused_computation.20.clone.1 | convolution fusion | flops 194281472 | bytes 8931841 | tf_op jit(solution)/shard_map/while/body/eval_jaxpr/kuv,klvc->luc/dot_general | solution.py:75
  282.2 0.8 reshape.166
  (80 shorter events, 9.8 us)
Async XLA Ops:
  2.9 33.9 %collective-permute-start = (f32[11,512]{1,0:T(8,128)S(1)}, f32[11,512]{1,0:T(8,128)S(1)}, u32[]{:S(2)}, u32[]{:S(2)}) collective-permute-start(f32[11,512]{1,0:T(8,128)S(1)} %get-tuple-element.135), channel_id=1, source_target_pairs={{0,2},{2,4},{4,6},{6,8},{8,10},{10,12},{12,14},{1,3},{3,5},{5,7},{... | collective-permute-start | bytes 67592 | tf_op jit(solution)/shard_map/ppermute | solution.py:20
  7.8 29.1 %collective-permute-start.1 = (f32[11,512]{1,0:T(8,128)S(1)}, f32[11,512]{1,0:T(8,128)S(1)}, u32[]{:S(2)}, u32[]{:S(2)}) collective-permute-start(f32[11,512]{1,0:T(8,128)S(1)} %get-tuple-element.136), channel_id=1, source_target_pairs={{2,0},{4,2},{6,4},{8,6},{10,8},{12,10},{14,12},{3,1},{5,3},{7,5},{... | collective-permute-start | bytes 67592 | tf_op jit(solution)/shard_map/ppermute | solution.py:23
  9.1 20.3 %all-to-all-start = ((s32[8,1,8]{2,1,0:T(1,128)}), s32[8,1,8]{2,1,0:T(1,128)S(1)}, u32[]{:S(2)}, u32[]{:S(2)}) async-start(s32[8,1,8]{2,1,0:T(1,128)} %bitcast.132), calls=%async_computation | async-start | bytes 8192 | tf_op jit(solution)/shard_map/all_to_all | solution.py:58
  20.6 0.8 copy-start.1
  20.8 7.8 %copy-start.9 = (s32[316,64]{0,1:T(8,128)S(1)}, s32[316,64]{0,1:T(8,128)}, u32[]{:S(2)}) copy-start(s32[316,64]{0,1:T(8,128)} %param.19) | copy-start | bytes 242692
  21.0 0.6 copy-start.4
  21.8 15.1 %copy-start.6 = (f32[3,2048]{1,0:T(4,128)S(1)}, f32[3,2048]{1,0:T(4,128)}, u32[]{:S(2)}) copy-start(f32[3,2048]{1,0:T(4,128)} %param.13) | copy-start | bytes 73732
  30.8 67.1 %all-to-all-start.1 = ((bf16[8,8,392]{2,1,0:T(8,128)(2,1)}), bf16[8,8,392]{2,1,0:T(8,128)(2,1)}, u32[]{:S(2)}, u32[]{:S(2)}) async-start(bf16[8,8,392]{2,1,0:T(8,128)(2,1)} %bitcast.18), calls=%async_computation.1 | async-start | bytes 131072 | tf_op jit(solution)/shard_map/all_to_all | solution.py:59
  67.6 6.2 %copy-start.3 = (f32[3,2,32,32]{3,2,1,0:T(8,128)S(1)}, f32[3,2,32,32]{3,2,1,0:T(8,128)}, u32[]{:S(2)}) copy-start(f32[3,2,32,32]{3,2,1,0:T(8,128)} %reshape.164) | copy-start | bytes 73732
  67.6 6.2 %copy-start.7 = (f32[2,8,32,32]{3,1,2,0:T(8,128)S(1)}, f32[2,8,32,32]{3,1,2,0:T(8,128)}, u32[]{:S(2)}) copy-start(f32[2,8,32,32]{3,1,2,0:T(8,128)} %custom-call.9) | copy-start | bytes 196612
  73.8 25.1 %copy-start.5 = (bf16[64,49,8]{0,2,1:T(8,128)(2,1)S(1)}, bf16[64,49,8]{0,2,1:T(8,128)(2,1)}, u32[]{:S(2)}) copy-start(bf16[64,49,8]{0,2,1:T(8,128)(2,1)} %copy-done.4) | copy-start | bytes 150532
  73.8 25.3 %copy-start = (f32[64,49,8]{0,1,2:T(8,128)S(1)}, f32[64,49,8]{0,1,2:T(8,128)}, u32[]{:S(2)}) copy-start(f32[64,49,8]{0,1,2:T(8,128)} %custom-call) | copy-start | bytes 301060
  99.2 182.6 %copy-start.2 = (bf16[49,2048]{0,1:T(8,128)(2,1)S(1)}, bf16[49,2048]{0,1:T(8,128)(2,1)}, u32[]{:S(2)}) copy-start(bf16[49,2048]{0,1:T(8,128)(2,1)} %copy-done.1) | copy-start | bytes 602116
  99.2 182.6 %copy-start.8 = (f32[64,32]{1,0:T(8,128)S(1)}, f32[64,32]{1,0:T(8,128)}, u32[]{:S(2)}) copy-start(f32[64,32]{1,0:T(8,128)} %get-tuple-element.137) | copy-start | bytes 24580
where the time goes:
time: 286 us; the launch traced here: 283 us
  local copies, waits for them, and re-layouts  225 us (79%)
  matrix products  34 us (12%)
  starting transfers between devices  19.1 us (7%)
  other arithmetic  3.87 us (1%)
    gather x8, local copies, waits for them, and re-layouts, accumulate(): combined[slot_table]  114 us
    reshape x4, local copies, waits for them, and re-layouts, accumulate(): combined[slot_table]  43.5 us
    dot_general x4, matrix products, accumulate(): jnp.einsum('kuv,klvc->luc', op_table, sources, preferred_element_type=jnp...  20 us
    dot_general x2, matrix products, near_tile(): jnp.einsum('nlij,cnlj->cli', kernel, nbr_charge, preferred_element_type=j...  13.4 us
    gather x2, local copies, waits for them, and re-layouts, per_device(): nbr_pos = extended[:3][:, near_lists]  9.43 us
    reshape x1, local copies, waits for them, and re-layouts, per_device(): nbr_charge.reshape(channel_count, neighbours, group_count, block_size, at...  9.42 us
    while x1, local copies, waits for them, and re-layouts, per_device(): near_parts = lax.map(near_tile, (target_blocks, pos_blocks, charge_blocks))  7.53 us
    all_to_all x1, starting transfers between devices, per_device(): lax.all_to_all(wanted, ('leaf', 'sub'), split_axis=0, concat_axis=0, tile...  6.97 us
  transfers between devices with their start and end apart: 4, of which 0 were waited for; matrix products, arithmetic and copies ran while one was open for 26% of the time, Pallas kernels for 0%

commit v1 on v0

v1 whole, which is shorter than its diff:
```python
import functools
import math

import jax
import jax.numpy as jnp
from jax import lax
from jax.experimental import pallas as pl
from jax.experimental.pallas import tpu as pltpu
from jax.sharding import PartitionSpec as P

HALO = 16
SOFT_SQ = 0.0625
NEAR_GAIN = 0.1
HALF = 64
STEP_TYPES = 16
NT = (((1,), (1,)), ((), ()))
F32 = jnp.float32
BF16 = jnp.bfloat16


def lane_iota(shape):
    return lax.broadcasted_iota(jnp.int32, shape, len(shape) - 1)


def chunk_mask(counts_ref, j, slots):
    shape = (8, 8 * slots)
    offset = lane_iota(shape) - slots * lax.broadcasted_iota(jnp.int32, shape, 0)
    counts = counts_ref[8 * j : 8 * j + 8, :]
    return (offset >= 0) & (offset < counts)


def fill_harmonics(harm_ref, harm2_ref):
    terms = harm_ref.shape[0]
    harm2_ref[...] = jnp.zeros_like(harm2_ref)
    harm2_ref[0:terms, :] = harm_ref[...]
    harm2_ref[HALF : HALF + terms, :] = harm_ref[...]


def compute_moments(charges_ref, counts_ref, harm2_ref, live_ref, mom_ref, leaves, slots):
    channels = charges_ref.shape[0]
    width = 8 * slots
    for j in range(leaves // 8):
        mask = chunk_mask(counts_ref, j, slots)
        q = charges_ref[:, j * width : (j + 1) * width].astype(F32)
        spread = jnp.where(mask[None], q[:, None, :], 0.0)
        live_ref[:, j * width : (j + 1) * width] = jnp.sum(spread, axis=1)
        m = lax.dot_general(
            spread.reshape(channels * 8, width).astype(BF16),
            harm2_ref[:, j * width : (j + 1) * width],
            NT,
            preferred_element_type=F32,
        )
        low = lane_iota((8, 128)) < HALF
        for pair in range(channels // 2):
            mom_ref[8 * j : 8 * j + 8, 128 * pair : 128 * pair + 128] = jnp.where(
                low, m[16 * pair : 16 * pair + 8], m[16 * pair + 8 : 16 * pair + 16]
            )


def build_rolled(window, rolled_ref, first_block):
    for b in range(window.shape[1] // 128):
        block = window[:, 128 * b : 128 * b + 128]
        for r in range(4):
            rolled_ref[r, first_block + b] = block if r == 0 else pltpu.roll(block, 32 * r, 1)


def compute_near(near_ref, rolled_ref, pos_ref, out_ref, leaves, slots, neighbours):
    groups = -(-neighbours // 4)
    last = rolled_ref.shape[1] - 1
    lane = lane_iota((16, 128))

    def body(g, carry):
        columns = pl.ds(pl.multiple_of(g * 128, 128), 128)
        targets = jnp.transpose(pos_ref[:, columns])
        kernels, charges = [], []
        for leaf in range(4):
            tgt = targets[32 * leaf : 32 * leaf + 32]
            tgt = [jnp.broadcast_to(tgt[:, k : k + 1], (32, 128)) for k in range(3)]
            k_parts, q_parts = [], []
            for n4 in range(groups):
                src = None
                for j in range(4):
                    n = 4 * n4 + j
                    if n < neighbours:
                        e = near_ref[n, g * 4 + leaf]
                        piece = rolled_ref[(j + 4 - e % 4) % 4, e // 4]
                    else:
                        piece = rolled_ref[0, last]
                    src = piece if src is None else jnp.where(lane >= 32 * j, piece, src)
                squared = None
                for k in range(3):
                    d = tgt[k] - src[8 + k : 9 + k]
                    squared = d * d if squared is None else squared + d * d
                k_parts.append(lax.rsqrt(squared + SOFT_SQ).astype(BF16))
                q_parts.append(src[0:8])
            kernels.append(jnp.concatenate(k_parts, axis=1))
            charges.append(jnp.concatenate(q_parts, axis=1))
        kernels = jnp.concatenate(kernels, axis=0)
        charges = jnp.concatenate(charges, axis=0).astype(BF16)
        full = lax.dot_general(charges, kernels, NT, preferred_element_type=F32)
        lane8 = lane_iota((8, 128))
        near = full[0:8]
        for leaf in range(1, 4):
            near = jnp.where(lane8 >= 32 * leaf, full[8 * leaf : 8 * leaf + 8], near)
        out_ref[:, columns] = near
        return carry

    lax.fori_loop(0, leaves // 4, body, 0)


def build_table(first, rows, value, table_ref, slots_pad):
    low = lane_iota((rows, 128)) < HALF
    for pair in range(value.shape[1] // 128):
        p = value[:, 128 * pair : 128 * pair + 128]
        r = pltpu.roll(p, HALF, 1)
        c0, c1 = 256 * pair, 256 * pair + 128
        table_ref[first : first + rows, c0 : c0 + 128] = jnp.where(low, p, 0.0).astype(BF16)
        table_ref[first : first + rows, c1 : c1 + 128] = jnp.where(low, r, 0.0).astype(BF16)
        second = slots_pad + first
        table_ref[second : second + rows, c0 : c0 + 128] = jnp.where(low, 0.0, r).astype(BF16)
        table_ref[second : second + rows, c1 : c1 + 128] = jnp.where(low, 0.0, p).astype(BF16)


def compute_local(index_ref, op_ref, table_ref, gathered_ref, acc_ref, leaves, channels):
    slots_pad = table_ref.shape[0] // 2
    pairs = STEP_TYPES // 2
    depth = STEP_TYPES * HALF
    acc_ref[...] = jnp.zeros_like(acc_ref)

    def body(step, carry):
        index = index_ref[step]
        lane = lane_iota((leaves, slots_pad))
        hot = []
        for pair in range(pairs):
            hot.append(
                jnp.concatenate(
                    [
                        jnp.where(index[:, t : t + 1] == lane, 1.0, 0.0).astype(BF16)
                        for t in (2 * pair, 2 * pair + 1)
                    ],
                    axis=1,
                )
            )
        hot = jnp.concatenate(hot, axis=0)
        for c2 in range(channels // 2):
            got = jnp.dot(
                hot, table_ref[:, 256 * c2 : 256 * c2 + 256], preferred_element_type=F32
            ).astype(BF16)
            for half in range(2):
                row = (2 * c2 + half) * leaves
                for pair in range(pairs):
                    gathered_ref[row : row + leaves, 128 * pair : 128 * pair + 128] = got[
                        leaves * pair : leaves * pair + leaves, 128 * half : 128 * half + 128
                    ]
        rows = pl.ds(pl.multiple_of(step * depth, depth), depth)
        acc_ref[...] += jnp.dot(gathered_ref[...], op_ref[rows, :], preferred_element_type=F32)
        return carry

    lax.fori_loop(0, index_ref.shape[0], body, 0)


def finish(acc_ref, harm2_ref, counts_ref, near_ref, out_ref, leaves, slots, channels):
    width = 8 * slots
    for j in range(leaves // 8):
        local = jnp.concatenate(
            [acc_ref[c * leaves + 8 * j : c * leaves + 8 * j + 8] for c in range(channels)], axis=0
        ).astype(BF16)
        columns = slice(j * width, (j + 1) * width)
        far = jnp.dot(local, harm2_ref[:, columns], preferred_element_type=F32)
        mask = chunk_mask(counts_ref, j, slots)
        far = jnp.sum(jnp.where(mask[None], far.reshape(channels, 8, width), 0.0), axis=1)
        alive = jnp.sum(jnp.where(mask, 1.0, 0.0), axis=0, keepdims=True)
        out_ref[:, columns] = far + (NEAR_GAIN * alive) * near_ref[:, columns]


def moments_kernel(dims, charges_ref, counts_ref, harm_ref, mom_ref, live_ref, harm2_ref, scratch):
    leaves, slots = dims
    fill_harmonics(harm_ref, harm2_ref)
    compute_moments(charges_ref, counts_ref, harm2_ref, live_ref, scratch, leaves, slots)
    mom_ref[...] = scratch[...].astype(BF16)


def main_kernel(
    dims, near_lists_ref, index_ref, op_ref, mom_ref, got_ref, window_ref, pos_ref, counts_ref,
    harm_ref, out_ref, harm2_ref, rolled_ref, near_ref, table_ref, gathered_ref, acc_ref,
):
    leaves, slots, channels, neighbours = dims
    fill_harmonics(harm_ref, harm2_ref)
    rolled_ref[:, rolled_ref.shape[1] - 1] = jnp.zeros((4, 16, 128), F32)
    build_rolled(window_ref[...], rolled_ref, 0)
    compute_near(near_lists_ref, rolled_ref, pos_ref, near_ref, leaves, slots, neighbours)
    slots_pad = table_ref.shape[0] // 2
    filled = leaves + got_ref.shape[0]
    if filled < slots_pad:
        for base in (0, slots_pad):
            table_ref[base + filled : base + slots_pad, :] = jnp.zeros(
                (slots_pad - filled, table_ref.shape[1]), BF16
            )
    build_table(0, leaves, mom_ref[...].astype(F32), table_ref, slots_pad)
    build_table(leaves, got_ref.shape[0], got_ref[...].astype(F32), table_ref, slots_pad)
    compute_local(index_ref, op_ref, table_ref, gathered_ref, acc_ref, leaves, channels)
    finish(acc_ref, harm2_ref, counts_ref, near_ref, out_ref, leaves, slots, channels)


def per_device(
    charges, positions, harmonics, operators, leaf_atoms, near_lists, requests, m2l_slots
):
    leaves = leaf_atoms.shape[1]
    atoms = positions.shape[1]
    slots = atoms // leaves
    terms = harmonics.shape[0]
    channels = charges.shape[1]
    types = operators.shape[0]
    neighbours = near_lists.shape[0]
    fetched = requests.shape[1] * requests.shape[2]
    slots_pad = -(-(leaves + fetched) // 128) * 128
    steps = -(-types // STEP_TYPES)
    types_pad = steps * STEP_TYPES
    counts = leaf_atoms.reshape(leaves, 1)
    vmem = pl.BlockSpec(memory_space=pltpu.VMEM)
    smem = pl.BlockSpec(memory_space=pltpu.SMEM)
    params = pltpu.CompilerParams(vmem_limit_bytes=48 * 1024 * 1024)

    moments, live = pl.pallas_call(
        functools.partial(moments_kernel, (leaves, slots)),
        out_shape=(
            jax.ShapeDtypeStruct((leaves, channels * HALF), BF16),
            jax.ShapeDtypeStruct((channels, atoms), F32),
        ),
        in_specs=[vmem] * 3,
        out_specs=(vmem, vmem),
        scratch_shapes=[pltpu.VMEM((128, atoms), BF16), pltpu.VMEM((leaves, channels * HALF), F32)],
        compiler_params=params,
    )(charges[0], counts, harmonics)

    axes = ("leaf", "sub")
    asked = lax.all_to_all(requests[0], axes, split_axis=0, concat_axis=0, tiled=True)
    got = lax.all_to_all(moments[asked], axes, split_axis=0, concat_axis=0, tiled=True)
    got = got.reshape(fetched, channels * HALF)
    stacked = jnp.concatenate(
        [live, positions, jnp.zeros((16 - channels - 3, atoms), F32)], axis=0
    )
    count = lax.axis_size(axes)
    forward = [(i, i + 1) for i in range(count - 1)]
    backward = [(t, s) for s, t in forward]
    width = HALO * slots
    low = lax.ppermute(stacked[:, atoms - width :], axes, forward)
    high = lax.ppermute(stacked[:, :width], axes, backward)
    window = jnp.concatenate([low, stacked, high], axis=1)
    index = jnp.pad(m2l_slots, ((0, types_pad - types), (0, 0)), constant_values=slots_pad)
    index = index.reshape(steps, STEP_TYPES, leaves).transpose(0, 2, 1)
    ops = jnp.pad(
        operators.transpose(0, 2, 1),
        ((0, types_pad - types), (0, HALF - terms), (0, 128 - terms)),
    ).reshape(types_pad * HALF, 128)

    pos8 = jnp.pad(positions, ((0, 5), (0, 0)))
    out = pl.pallas_call(
        functools.partial(main_kernel, (leaves, slots, channels, neighbours)),
        out_shape=jax.ShapeDtypeStruct((channels, atoms), F32),
        in_specs=[smem] + [vmem] * 8,
        out_specs=vmem,
        scratch_shapes=[
            pltpu.VMEM((128, atoms), BF16),
            pltpu.VMEM((4, window.shape[1] // 128 + 1, 16, 128), F32),
            pltpu.VMEM((channels, atoms), F32),
            pltpu.VMEM((2 * slots_pad, channels * 128), BF16),
            pltpu.VMEM((channels * leaves, STEP_TYPES * HALF), BF16),
            pltpu.VMEM((channels * leaves, 128), F32),
        ],
        compiler_params=params,
    )(near_lists, index, ops, moments, got, window, pos8, counts, harmonics)
    return out[None]


def solution(mesh):
    return jax.shard_map(
        per_device,
        mesh=mesh,
        in_specs=(
            P("chan", None, ("groups", "leaf", "sub")),
            P(None, ("groups", "leaf", "sub")),
            P(None, ("groups", "leaf", "sub")),
            P(),
            P(("groups", "leaf", "sub"), None),
            P(None, ("groups", "leaf", "sub")),
            P(("groups", "leaf", "sub"), None, None),
            P(None, ("groups", "leaf", "sub")),
        ),
        out_specs=P("chan", None, ("groups", "leaf", "sub")),
        check_vma=False,
    )
```

time: 286 us -> 90.8 us (0.32)
  local copies, waits for them, and re-layouts: 225 us -> 22.6 us
  Pallas kernels: 0 us -> 40.9 us
  matrix products: 34 us -> 0 us
  waiting for transfers between devices: 0.01 us -> 6.85 us
  other arithmetic: 3.87 us -> 0.77 us
    gather x12 -> x1, local copies, waits for them, and re-layouts: 131 us -> 1.33 us  [per_device(): moments[asked]]
    reshape x12 -> x2, local copies, waits for them, and re-layouts: 64.8 us -> 0.98 us  [the longest x1 0.74 us: per_device(): counts = leaf_atoms.reshape(leaves, 1)]
    pallas_call x0 -> x2, Pallas kernels: none -> 40.9 us  [the longest x1 40.5 us: per_device(): pl.pallas_call(functools.partial(main_kernel, (leaves, slots, channels, n...]
    dot_general x8 -> x0, matrix products: 34 us -> none  [the longest x4 20 us: accumulate(): jnp.einsum('kuv,klvc->luc', op_table, sources, preferred_element_type=jnp...]
    while x7 -> x0, local copies, waits for them, and re-layouts: 11.7 us -> none  [the longest x1 7.53 us: per_device(): near_parts = lax.map(near_tile, (target_blocks, pos_blocks, charge_blocks))]
    unnamed x23 -> x14, local copies, waits for them, and re-layouts: 3.96 us -> 13.3 us
    slice x6 -> x0, local copies, waits for them, and re-layouts: 7.88 us -> none  [the longest x2 6.29 us: near_tile(): nbr_pos[coordinate][:, :, None, :]]
    pad x0 -> x3, local copies, waits for them, and re-layouts: none -> 6.91 us  [the longest x1 6.12 us: per_device(): jnp.pad(operators.transpose(0, 2, 1), ((0, types_pad - types), (0, HALF -...]
  transfers between devices with their start and end apart: 4 -> 4, of which waited for: 0 -> 1; matrix products, arithmetic and copies ran while one was open for 26% -> 22% of each run, Pallas kernels for 0% -> 0%
where the time goes in v1:
time: 90.8 us; the launch traced here: 90.3 us
  Pallas kernels  40.9 us (45%)
  local copies, waits for them, and re-layouts  22.6 us (25%)
  starting transfers between devices  19.1 us (21%)
  waiting for transfers between devices  6.85 us (8%)
    pallas_call x1, Pallas kernels, per_device(): pl.pallas_call(functools.partial(main_kernel, (leaves, slots, channels, n...  40.5 us
    unnamed x14, local copies, waits for them, and re-layouts  13.3 us
    all_to_all x1, starting transfers between devices, per_device(): lax.all_to_all(requests[0], axes, split_axis=0, concat_axis=0, tiled=True)  6.97 us
    all_to_all x1, waiting for transfers between devices, per_device(): lax.all_to_all(moments[asked], axes, split_axis=0, concat_axis=0, tiled=T...  6.85 us
    pad x1, local copies, waits for them, and re-layouts, per_device(): jnp.pad(operators.transpose(0, 2, 1), ((0, types_pad - types), (0, HALF -...  6.12 us
    all_to_all x1, starting transfers between devices, per_device(): lax.all_to_all(moments[asked], axes, split_axis=0, concat_axis=0, tiled=T...  6 us
    ppermute x1, starting transfers between devices, per_device(): low = lax.ppermute(stacked[:, atoms - width:], axes, forward)  4.84 us
  transfers between devices with their start and end apart: 4, of which 1 were waited for; matrix products, arithmetic and copies ran while one was open for 22% of the time, Pallas kernels for 0%

profile of v1, /device:TPU:0, one launch (start us, length us, event | category | flops | bytes accessed | tf_op | source)
XLA Modules:
  0.0 90.3 jit_solution(9405534714965172522)
XLA Ops:
  0.0 0.7 copy.20.counts_ref
  0.7 0.0 copy-start
  0.7 0.9 %copy-done = bf16[49,2048]{1,0:T(8,128)(2,1)S(1)} copy-done((bf16[49,2048]{1,0:T(8,128)(2,1)S(1)}, bf16[49,2048]{1,0:T(8,128)(2,1)}, u32[]{:S(2)}) %copy-start) | copy-done | bytes 200728
  1.7 0.0 copy-start.2
  1.7 0.8 copy-done.2
  2.4 0.0 copy-start.5
  2.4 0.4 shard_map.82
  2.9 0.7 pad_maximum_fusion.3
  3.6 4.8 %collective-permute-start = (f32[16,512]{1,0:T(8,128)S(1)}, f32[16,512]{1,0:T(8,128)S(1)}, u32[]{:S(2)}, u32[]{:S(2)}) collective-permute-start(f32[16,512]{1,0:T(8,128)S(1)} %get-tuple-element.9), channel_id=1, source_target_pairs={{0,2},{2,4},{4,6},{6,8},{8,10},{10,12},{12,14},{1,3},{3,5},{5,7},{... | collective-permute-start | bytes 98312 | tf_op jit(solution)/shard_map/ppermute | solution.py:247
  8.4 1.3 %collective-permute-start.1 = (f32[16,512]{1,0:T(8,128)S(1)}, f32[16,512]{1,0:T(8,128)S(1)}, u32[]{:S(2)}, u32[]{:S(2)}) collective-permute-start(f32[16,512]{1,0:T(8,128)S(1)} %get-tuple-element.10), channel_id=1, source_target_pairs={{2,0},{4,2},{6,4},{8,6},{10,8},{12,10},{14,12},{3,1},{5,3},{7,5},{... | collective-permute-start | bytes 98312 | tf_op jit(solution)/shard_map/ppermute | solution.py:248
  9.7 7.0 %all-to-all-start = ((s32[8,1,8]{2,1,0:T(1,128)}), s32[8,1,8]{2,1,0:T(1,128)S(1)}, u32[]{:S(2)}, u32[]{:S(2)}) async-start(s32[8,1,8]{2,1,0:T(1,128)} %bitcast.22), calls=%async_computation | async-start | bytes 8192 | tf_op jit(solution)/shard_map/all_to_all | solution.py:237
  16.7 0.8 pad.14.pos_ref
  17.5 11.4 %copy.23 = bf16[316,49,49]{2,1,0:T(8,128)(2,1)} copy(bf16[316,49,49]{0,1,2:T(8,128)(2,1)} %bitcast.19) | data formatting | bytes 3034864
  28.9 0.0 copy-done.5
  28.9 0.1 copy.17
  29.1 0.2 copy.18
  29.3 0.0 copy-start.4
  29.3 0.0 copy-start.1
  29.3 0.0 copy-start.3
  29.3 6.1 %pad.13.clone = bf16[320,64,128]{2,1,0:T(8,128)(2,1)} pad(bf16[316,49,49]{2,1,0:T(8,128)(2,1)} %copy.23, bf16[]{:T(256)} %constant.3.clone.1), padding=0_4x0_15x0_79 | pad | bytes 6760314 | tf_op jit(solution)/shard_map/jit(_pad)/pad | solution.py:252
  35.5 0.0 all-to-all-done
  35.5 0.1 reshape.49
  35.6 1.3 %gather_fusion = bf16[64,512]{1,0:T(8,128)(2,1)} fusion(bf16[64,512]{1,0:T(8,128)(2,1)S(1)} %get-tuple-element.7.mom_ref, s32[1024]{0:T(1024)S(1)} %pad_clamp_fusion), kind=kCustom, calls=%fused_computation | custom fusion | bytes 131328 | tf_op jit(solution)/shard_map/gather | solution.py:238
  36.9 6.0 %all-to-all-start.1 = ((bf16[8,8,512]{2,1,0:T(8,128)(2,1)}), bf16[8,8,512]{2,1,0:T(8,128)(2,1)S(1)}, u32[]{:S(2)}, u32[]{:S(2)}) async-start(bf16[8,8,512]{2,1,0:T(8,128)(2,1)} %bitcast.9), calls=%async_computation.1 | async-start | bytes 131072 | tf_op jit(solution)/shard_map/all_to_all | solution.py:238
  42.9 0.0 collective-permute-done
  42.9 0.0 collective-permute-done.1
  42.9 0.0 copy-done.4
  42.9 6.8 %all-to-all-done.1 = bf16[8,8,512]{2,1,0:T(8,128)(2,1)S(1)} async-done(((bf16[8,8,512]{2,1,0:T(8,128)(2,1)}), bf16[8,8,512]{2,1,0:T(8,128)(2,1)S(1)}, u32[]{:S(2)}, u32[]{:S(2)}) %all-to-all-start.1) | async-done | bytes 65568 | tf_op jit(solution)/shard_map/all_to_all | solution.py:238
  49.8 0.0 copy-done.1
  49.8 0.0 copy-done.3
  49.8 40.5 %shard_map.83 = f32[8,2048]{1,0:T(8,128)} custom-call(s32[27,64]{1,0:T(8,128)S(1)} %copy-done.3, s32[20,64,16]{2,1,0:T(8,128)S(1)} %bitcast.15, bf16[20480,128]{1,0:T(8,128)(2,1)} %bitcast.18, bf16[64,512]{1,0:T(8,128)(2,1)S(1)} %get-tuple-element.7.mom_ref, bf16[64,512]{1,0:T(8,128)(2,1)S(1)} %bitcast.16, f32[16,3072]{1,0:T(8,128)S(1)} %pad_maximum_fusion.window_ref, ...), custom_call_target="tpu_custom_call" | custom-call | tf_op jit(solution)/shard_map/pallas_call | solution.py:258
  (5 shorter events, 0.1 us)
Async XLA Ops:
  0.7 0.9 %copy-start = (bf16[49,2048]{1,0:T(8,128)(2,1)S(1)}, bf16[49,2048]{1,0:T(8,128)(2,1)}, u32[]{:S(2)}) copy-start(bf16[49,2048]{1,0:T(8,128)(2,1)} %harm_ref.3) | copy-start | bytes 602116
  1.7 0.8 copy-start.2
  2.4 26.5 %copy-start.5 = (s32[316,64]{0,1:T(8,128)S(1)}, s32[316,64]{0,1:T(8,128)}, u32[]{:S(2)}) copy-start(s32[316,64]{0,1:T(8,128)} %param.15) | copy-start | bytes 242692
  3.6 39.3 %collective-permute-start = (f32[16,512]{1,0:T(8,128)S(1)}, f32[16,512]{1,0:T(8,128)S(1)}, u32[]{:S(2)}, u32[]{:S(2)}) collective-permute-start(f32[16,512]{1,0:T(8,128)S(1)} %get-tuple-element.9), channel_id=1, source_target_pairs={{0,2},{2,4},{4,6},{6,8},{8,10},{10,12},{12,14},{1,3},{3,5},{5,7},{... | collective-permute-start | bytes 98312 | tf_op jit(solution)/shard_map/ppermute | solution.py:247
  8.4 34.5 %collective-permute-start.1 = (f32[16,512]{1,0:T(8,128)S(1)}, f32[16,512]{1,0:T(8,128)S(1)}, u32[]{:S(2)}, u32[]{:S(2)}) collective-permute-start(f32[16,512]{1,0:T(8,128)S(1)} %get-tuple-element.10), channel_id=1, source_target_pairs={{2,0},{4,2},{6,4},{8,6},{10,8},{12,10},{14,12},{3,1},{5,3},{7,5},{... | collective-permute-start | bytes 98312 | tf_op jit(solution)/shard_map/ppermute | solution.py:248
  9.7 25.7 %all-to-all-start = ((s32[8,1,8]{2,1,0:T(1,128)}), s32[8,1,8]{2,1,0:T(1,128)S(1)}, u32[]{:S(2)}, u32[]{:S(2)}) async-start(s32[8,1,8]{2,1,0:T(1,128)} %bitcast.22), calls=%async_computation | async-start | bytes 8192 | tf_op jit(solution)/shard_map/all_to_all | solution.py:237
  29.3 13.6 %copy-start.4 = (f32[3,2048]{1,0:T(4,128)S(1)}, f32[3,2048]{1,0:T(4,128)}, u32[]{:S(2)}) copy-start(f32[3,2048]{1,0:T(4,128)} %param.9) | copy-start | bytes 73732
  29.3 20.5 %copy-start.1 = (bf16[49,2048]{1,0:T(8,128)(2,1)S(1)}, bf16[49,2048]{1,0:T(8,128)(2,1)}, u32[]{:S(2)}) copy-start(bf16[49,2048]{1,0:T(8,128)(2,1)} %harm_ref.3) | copy-start | bytes 602116
  29.3 20.5 %copy-start.3 = (s32[27,64]{1,0:T(8,128)S(1)}, s32[27,64]{1,0:T(8,128)}, u32[]{:S(2)}) copy-start(s32[27,64]{1,0:T(8,128)} %near_lists_ref.1) | copy-start | bytes 20740
  36.9 12.9 %all-to-all-start.1 = ((bf16[8,8,512]{2,1,0:T(8,128)(2,1)}), bf16[8,8,512]{2,1,0:T(8,128)(2,1)S(1)}, u32[]{:S(2)}, u32[]{:S(2)}) async-start(bf16[8,8,512]{2,1,0:T(8,128)(2,1)} %bitcast.9), calls=%async_computation.1 | async-start | bytes 131072 | tf_op jit(solution)/shard_map/all_to_all | solution.py:238

commit v2 on v1

--- a/solution.py
+++ b/solution.py
@@ -12,7 +12,6 @@
 SOFT_SQ = 0.0625
 NEAR_GAIN = 0.1
 HALF = 64
-STEP_TYPES = 16
 NT = (((1,), (1,)), ((), ()))
 F32 = jnp.float32
 BF16 = jnp.bfloat16
@@ -108,55 +107,46 @@
     lax.fori_loop(0, leaves // 4, body, 0)
 
 
-def build_table(first, rows, value, table_ref, slots_pad):
-    low = lane_iota((rows, 128)) < HALF
-    for pair in range(value.shape[1] // 128):
-        p = value[:, 128 * pair : 128 * pair + 128]
-        r = pltpu.roll(p, HALF, 1)
-        c0, c1 = 256 * pair, 256 * pair + 128
-        table_ref[first : first + rows, c0 : c0 + 128] = jnp.where(low, p, 0.0).astype(BF16)
-        table_ref[first : first + rows, c1 : c1 + 128] = jnp.where(low, r, 0.0).astype(BF16)
-        second = slots_pad + first
-        table_ref[second : second + rows, c0 : c0 + 128] = jnp.where(low, 0.0, r).astype(BF16)
-        table_ref[second : second + rows, c1 : c1 + 128] = jnp.where(low, 0.0, p).astype(BF16)
-
-
-def compute_local(index_ref, op_ref, table_ref, gathered_ref, acc_ref, leaves, channels):
-    slots_pad = table_ref.shape[0] // 2
-    pairs = STEP_TYPES // 2
-    depth = STEP_TYPES * HALF
+def gather_lanes(row, index):
+    return jnp.take_along_axis(row, index, axis=1, mode="promise_in_bounds")
+
+
+def compute_local(index_ref, op_ref, table_ref, acc_ref, leaves, channels):
+    terms, _, types_pad = op_ref.shape
+    blocks = table_ref.shape[0]
+    batch = math.gcd(terms, 7)
     acc_ref[...] = jnp.zeros_like(acc_ref)
 
     def body(step, carry):
-        index = index_ref[step]
-        lane = lane_iota((leaves, slots_pad))
-        hot = []
-        for pair in range(pairs):
-            hot.append(
-                jnp.concatenate(
-                    [
-                        jnp.where(index[:, t : t + 1] == lane, 1.0, 0.0).astype(BF16)
-                        for t in (2 * pair, 2 * pair + 1)
-                    ],
-                    axis=1,
-                )
-            )
-        hot = jnp.concatenate(hot, axis=0)
-        for c2 in range(channels // 2):
-            got = jnp.dot(
-                hot, table_ref[:, 256 * c2 : 256 * c2 + 256], preferred_element_type=F32
-            ).astype(BF16)
-            for half in range(2):
-                row = (2 * c2 + half) * leaves
-                for pair in range(pairs):
-                    gathered_ref[row : row + leaves, 128 * pair : 128 * pair + 128] = got[
-                        leaves * pair : leaves * pair + leaves, 128 * half : 128 * half + 128
-                    ]
-        rows = pl.ds(pl.multiple_of(step * depth, depth), depth)
-        acc_ref[...] += jnp.dot(gathered_ref[...], op_ref[rows, :], preferred_element_type=F32)
+        parts = []
+        for k in range(batch):
+            v = step * batch + k
+            rows = []
+            for c in range(channels):
+                lines = [
+                    jnp.broadcast_to(table_ref[b, pl.ds(c * HALF + v, 1), :], (8, 128))
+                    for b in range(blocks)
+                ]
+                for l8 in range(leaves // 8):
+                    columns = []
+                    for t in range(types_pad // 128):
+                        index = index_ref[8 * l8 : 8 * l8 + 8, 128 * t : 128 * t + 128]
+                        if blocks == 1:
+                            got = gather_lanes(lines[0], index)
+                        else:
+                            got = jnp.zeros((8, 128), F32)
+                            for b in range(blocks):
+                                piece = gather_lanes(lines[b], index % 128)
+                                got = jnp.where(index // 128 == b, piece, got)
+                        columns.append(got)
+                    rows.append(jnp.concatenate(columns, axis=1))
+            parts.append(jnp.concatenate(rows, axis=0).astype(BF16))
+        sources = jnp.concatenate(parts, axis=1)
+        ops = jnp.concatenate([op_ref[step * batch + k] for k in range(batch)], axis=1)
+        acc_ref[...] += lax.dot_general(sources, ops, NT, preferred_element_type=F32)
         return carry
 
-    lax.fori_loop(0, index_ref.shape[0], body, 0)
+    lax.fori_loop(0, terms // batch, body, 0)
 
 
 def finish(acc_ref, harm2_ref, counts_ref, near_ref, out_ref, leaves, slots, channels):
@@ -166,7 +156,7 @@
             [acc_ref[c * leaves + 8 * j : c * leaves + 8 * j + 8] for c in range(channels)], axis=0
         ).astype(BF16)
         columns = slice(j * width, (j + 1) * width)
-        far = jnp.dot(local, harm2_ref[:, columns], preferred_element_type=F32)
+        far = jnp.dot(local, harm2_ref[0:HALF, columns], preferred_element_type=F32)
         mask = chunk_mask(counts_ref, j, slots)
         far = jnp.sum(jnp.where(mask[None], far.reshape(channels, 8, width), 0.0), axis=1)
         alive = jnp.sum(jnp.where(mask, 1.0, 0.0), axis=0, keepdims=True)
@@ -180,25 +170,26 @@
     mom_ref[...] = scratch[...].astype(BF16)
 
 
-def main_kernel(
-    dims, near_lists_ref, index_ref, op_ref, mom_ref, got_ref, window_ref, pos_ref, counts_ref,
-    harm_ref, out_ref, harm2_ref, rolled_ref, near_ref, table_ref, gathered_ref, acc_ref,
-):
+def near_kernel(dims, near_lists_ref, window_ref, pos_ref, near_ref, rolled_ref):
     leaves, slots, channels, neighbours = dims
-    fill_harmonics(harm_ref, harm2_ref)
     rolled_ref[:, rolled_ref.shape[1] - 1] = jnp.zeros((4, 16, 128), F32)
     build_rolled(window_ref[...], rolled_ref, 0)
     compute_near(near_lists_ref, rolled_ref, pos_ref, near_ref, leaves, slots, neighbours)
-    slots_pad = table_ref.shape[0] // 2
-    filled = leaves + got_ref.shape[0]
-    if filled < slots_pad:
-        for base in (0, slots_pad):
-            table_ref[base + filled : base + slots_pad, :] = jnp.zeros(
-                (slots_pad - filled, table_ref.shape[1]), BF16
+
+
+def far_kernel(
+    dims, index_ref, op_ref, sources_ref, near_ref, counts_ref, harm_ref, out_ref, harm2_ref,
+    table_ref, acc_ref,
+):
+    leaves, slots, channels = dims
+    fill_harmonics(harm_ref, harm2_ref)
+    for b in range(table_ref.shape[0]):
+        block = sources_ref[128 * b : 128 * b + 128, :].astype(F32)
+        for p in range(block.shape[1] // 128):
+            table_ref[b, 128 * p : 128 * p + 128, :] = jnp.transpose(
+                block[:, 128 * p : 128 * p + 128]
             )
-    build_table(0, leaves, mom_ref[...].astype(F32), table_ref, slots_pad)
-    build_table(leaves, got_ref.shape[0], got_ref[...].astype(F32), table_ref, slots_pad)
-    compute_local(index_ref, op_ref, table_ref, gathered_ref, acc_ref, leaves, channels)
+    compute_local(index_ref, op_ref, table_ref, acc_ref, leaves, channels)
     finish(acc_ref, harm2_ref, counts_ref, near_ref, out_ref, leaves, slots, channels)
 
 
@@ -214,8 +205,7 @@
     neighbours = near_lists.shape[0]
     fetched = requests.shape[1] * requests.shape[2]
     slots_pad = -(-(leaves + fetched) // 128) * 128
-    steps = -(-types // STEP_TYPES)
-    types_pad = steps * STEP_TYPES
+    types_pad = -(-types // 128) * 128
     counts = leaf_atoms.reshape(leaves, 1)
     vmem = pl.BlockSpec(memory_space=pltpu.VMEM)
     smem = pl.BlockSpec(memory_space=pltpu.SMEM)
@@ -247,29 +237,44 @@
     low = lax.ppermute(stacked[:, atoms - width :], axes, forward)
     high = lax.ppermute(stacked[:, :width], axes, backward)
     window = jnp.concatenate([low, stacked, high], axis=1)
-    index = jnp.pad(m2l_slots, ((0, types_pad - types), (0, 0)), constant_values=slots_pad)
-    index = index.reshape(steps, STEP_TYPES, leaves).transpose(0, 2, 1)
+    me = lax.axis_index(axes)
+    capacity = requests.shape[2]
+    spare = leaves + capacity * me
+    index = jnp.where(m2l_slots < leaves + fetched, m2l_slots, spare).T
+    index = jnp.pad(index, ((0, 0), (0, types_pad - types)))
     ops = jnp.pad(
-        operators.transpose(0, 2, 1),
-        ((0, types_pad - types), (0, HALF - terms), (0, 128 - terms)),
-    ).reshape(types_pad * HALF, 128)
-
+        operators.transpose(2, 1, 0), ((0, 0), (0, HALF - terms), (0, types_pad - types))
+    )
+    own = jnp.arange(fetched)[:, None] // capacity == me
+    sources = jnp.concatenate(
+        [
+            moments,
+            jnp.where(own, 0, got),
+            jnp.zeros((slots_pad - leaves - fetched, channels * HALF), BF16),
+        ],
+        axis=0,
+    )
     pos8 = jnp.pad(positions, ((0, 5), (0, 0)))
+    near = pl.pallas_call(
+        functools.partial(near_kernel, (leaves, slots, channels, neighbours)),
+        out_shape=jax.ShapeDtypeStruct((channels, atoms), F32),
+        in_specs=[smem] + [vmem] * 2,
+        out_specs=vmem,
+        scratch_shapes=[pltpu.VMEM((4, window.shape[1] // 128 + 1, 16, 128), F32)],
+        compiler_params=params,
+    )(near_lists, window, pos8)
     out = pl.pallas_call(
-        functools.partial(main_kernel, (leaves, slots, channels, neighbours)),
+        functools.partial(far_kernel, (leaves, slots, channels)),
         out_shape=jax.ShapeDtypeStruct((channels, atoms), F32),
-        in_specs=[smem] + [vmem] * 8,
+        in_specs=[vmem] * 6,
         out_specs=vmem,
         scratch_shapes=[
             pltpu.VMEM((128, atoms), BF16),
-            pltpu.VMEM((4, window.shape[1] // 128 + 1, 16, 128), F32),
-            pltpu.VMEM((channels, atoms), F32),
-            pltpu.VMEM((2 * slots_pad, channels * 128), BF16),
-            pltpu.VMEM((channels * leaves, STEP_TYPES * HALF), BF16),
-            pltpu.VMEM((channels * leaves, 128), F32),
+            pltpu.VMEM((slots_pad // 128, channels * HALF, 128), F32),
+            pltpu.VMEM((channels * leaves, HALF), F32),
         ],
         compiler_params=params,
-    )(near_lists, index, ops, moments, got, window, pos8, counts, harmonics)
+    )(index, ops, sources, near, counts, harmonics)
     return out[None]
 
 

time: 90.8 us -> 65.6 us (0.72)
  local copies, waits for them, and re-layouts: 22.6 us -> 6.97 us
  waiting for transfers between devices: 6.85 us -> 0.01 us
  Pallas kernels: 40.9 us -> 37 us
  other arithmetic: 0.77 us -> 1.77 us
    unnamed x14 -> x11, local copies, waits for them, and re-layouts: 13.3 us -> 3.59 us
    all_to_all x1, waiting for transfers between devices: 6.85 us -> 0.01 us  [per_device(): lax.all_to_all(moments[asked], axes, split_axis=0, concat_axis=0, tiled=T...]
    pad x2, local copies, waits for them, and re-layouts: 6.14 us -> 0.44 us  [the longest x1 0.43 us: per_device(): jnp.pad(operators.transpose(2, 1, 0), ((0, 0), (0, HALF - terms), (0, typ...]
    pallas_call x1 -> x2, Pallas kernels: 40.5 us -> 36.6 us  [the longest x1 20.8 us: per_device(): pl.pallas_call(functools.partial(near_kernel, (leaves, slots, channels, n...]
  transfers between devices with their start and end apart: 4 -> 4, of which waited for: 1 -> 0; matrix products, arithmetic and copies ran while one was open for 22% -> 11% of each run, Pallas kernels for 0% -> 33%
where the time goes in v2:
time: 65.6 us; the launch traced here: 65.1 us
  Pallas kernels  37 us (56%)
  starting transfers between devices  19.1 us (29%)
  local copies, waits for them, and re-layouts  6.97 us (11%)
  other arithmetic  1.77 us (3%)
    pallas_call x1, Pallas kernels, per_device(): pl.pallas_call(functools.partial(near_kernel, (leaves, slots, channels, n...  20.8 us
    pallas_call x1, Pallas kernels, per_device(): pl.pallas_call(functools.partial(far_kernel, (leaves, slots, channels)),...  15.8 us
    all_to_all x1, starting transfers between devices, per_device(): lax.all_to_all(requests[0], axes, split_axis=0, concat_axis=0, tiled=True)  7.25 us
    all_to_all x1, starting transfers between devices, per_device(): lax.all_to_all(moments[asked], axes, split_axis=0, concat_axis=0, tiled=T...  5.99 us
    ppermute x1, starting transfers between devices, per_device(): low = lax.ppermute(stacked[:, atoms - width:], axes, forward)  4.55 us
    unnamed x11, local copies, waits for them, and re-layouts  3.59 us
    gather x1, local copies, waits for them, and re-layouts, per_device(): moments[asked]  1.33 us
  transfers between devices with their start and end apart: 4, of which 0 were waited for; matrix products, arithmetic and copies ran while one was open for 11% of the time, Pallas kernels for 33%

profile of v2, /device:TPU:0, one launch (start us, length us, event | category | flops | bytes accessed | tf_op | source)
XLA Modules:
  0.0 65.1 jit_solution(12552522518518917875)
XLA Ops:
  0.0 7.3 %all-to-all-start = ((s32[8,1,8]{2,1,0:T(1,128)}), s32[8,1,8]{2,1,0:T(1,128)S(1)}, u32[]{:S(2)}, u32[]{:S(2)}) async-start(s32[8,1,8]{2,1,0:T(1,128)} %bitcast.20), calls=%async_computation | async-start | bytes 8192 | tf_op jit(solution)/shard_map/all_to_all | solution.py:227
  7.3 0.7 %copy.13.counts_ref = s32[64,1]{1,0:T(8,128)S(1)} copy(s32[64,1]{0,1:T(1,128)} %bitcast.21) | data formatting | bytes 512 | tf_op jit(solution)/shard_map/reshape | solution.py:209
  8.0 0.0 copy-start
  8.0 0.9 %copy-done = bf16[49,2048]{1,0:T(8,128)(2,1)S(1)} copy-done((bf16[49,2048]{1,0:T(8,128)(2,1)S(1)}, bf16[49,2048]{1,0:T(8,128)(2,1)}, u32[]{:S(2)}) %copy-start) | copy-done | bytes 200728
  8.9 0.0 copy-start.2
  8.9 0.8 %copy-done.2 = bf16[1,8,2048]{2,1,0:T(8,128)(2,1)S(1)} copy-done((bf16[1,8,2048]{2,1,0:T(8,128)(2,1)S(1)}, bf16[1,8,2048]{2,1,0:T(8,128)(2,1)}, u32[]{:S(2)}) %copy-start.2) | copy-done | bytes 32792
  9.7 0.4 shard_map.82
  10.1 0.7 %pad_maximum_fusion.4 = (f32[16,512]{1,0:T(8,128)S(1)}, f32[16,512]{1,0:T(8,128)S(1)}) fusion(f32[5,2048]{1,0:T(8,128)S(1)} %broadcast_in_dim.27, f32[3,2048]{1,0:T(4,128)} %param.9, f32[8,2048]{1,0:T(8,128)S(1)} %get-tuple-element.8), kind=kLoop, calls=%fused_computation.9 | loop fusion | flops 32768 | bytes 196608 | tf_op jit(solution)/shard_map/slice | solution.py:237
  10.8 1.3 %collective-permute-start.1 = (f32[16,512]{1,0:T(8,128)S(1)}, f32[16,512]{1,0:T(8,128)S(1)}, u32[]{:S(2)}, u32[]{:S(2)}) collective-permute-start(f32[16,512]{1,0:T(8,128)S(1)} %get-tuple-element.10), channel_id=1, source_target_pairs={{2,0},{4,2},{6,4},{8,6},{10,8},{12,10},{14,12},{3,1},{5,3},{7,5},{... | collective-permute-start | bytes 98312 | tf_op jit(solution)/shard_map/ppermute | solution.py:238
  12.1 4.6 %collective-permute-start = (f32[16,512]{1,0:T(8,128)S(1)}, f32[16,512]{1,0:T(8,128)S(1)}, u32[]{:S(2)}, u32[]{:S(2)}) collective-permute-start(f32[16,512]{1,0:T(8,128)S(1)} %get-tuple-element.9), channel_id=1, source_target_pairs={{0,2},{2,4},{4,6},{6,8},{8,10},{10,12},{12,14},{1,3},{3,5},{5,7},{... | collective-permute-start | bytes 98312 | tf_op jit(solution)/shard_map/ppermute | solution.py:237
  16.7 0.9 %fusion = s32[64,316]{1,0:T(8,128)S(1)} fusion(s32[316,64]{0,1:T(8,128)} %param.15, s32[]{:T(128)S(6)} %add.32), kind=kLoop, calls=%fused_computation.5 | loop fusion | flops 40448 | bytes 161796 | tf_op jit(solution)/shard_map/transpose | solution.py:243
  17.6 0.8 %pad.14.pos_ref = f32[8,2048]{1,0:T(8,128)S(1)} pad(f32[3,2048]{1,0:T(4,128)} %param.9, f32[]{:T(128)} %constant.41.clone.1), padding=0_5x0_0 | pad | bytes 90116 | tf_op jit(solution)/shard_map/jit(_pad)/pad | solution.py:257
  18.4 1.9 %copy.17 = bf16[316,49,49]{0,1,2:T(8,128)(2,1)S(1)} copy(bf16[316,49,49]{0,2,1:T(8,128)(2,1)} %param.11) | data formatting | bytes 3034864 | tf_op args[3]
  20.3 0.0 copy-start.4
  20.3 0.0 copy-start.3
  20.3 0.0 copy-start.1
  20.3 0.4 pad.13.op_ref
  20.8 0.0 all-to-all-done
  20.8 0.1 reshape.80
  20.9 1.3 %gather_fusion = bf16[64,512]{1,0:T(8,128)(2,1)} fusion(bf16[64,512]{1,0:T(8,128)(2,1)S(1)} %get-tuple-element.7, s32[1024]{0:T(1024)S(1)} %pad_clamp_fusion), kind=kCustom, calls=%fused_computation | custom fusion | bytes 131328 | tf_op jit(solution)/shard_map/gather | solution.py:228
  22.2 6.0 %all-to-all-start.1 = ((bf16[8,8,512]{2,1,0:T(8,128)(2,1)}), bf16[8,8,512]{2,1,0:T(8,128)(2,1)S(1)}, u32[]{:S(2)}, u32[]{:S(2)}) async-start(bf16[8,8,512]{2,1,0:T(8,128)(2,1)} %bitcast.7), calls=%async_computation.1 | async-start | bytes 131072 | tf_op jit(solution)/shard_map/all_to_all | solution.py:228
  28.2 0.0 collective-permute-done.1
  28.2 0.0 collective-permute-done
  28.2 0.0 copy-done.4
  28.3 0.0 copy-done.3
  28.3 20.8 %shard_map.83.near_ref = f32[8,2048]{1,0:T(8,128)S(1)} custom-call(s32[27,64]{1,0:T(8,128)S(1)} %copy-done.3, f32[16,3072]{1,0:T(8,128)S(1)} %pad_maximum_fusion.window_ref, f32[8,2048]{1,0:T(8,128)S(1)} %pad.14.pos_ref), custom_call_target="tpu_custom_call" | custom-call | tf_op jit(solution)/shard_map/pallas_call | solution.py:258
  49.1 0.0 all-to-all-done.1
  49.1 0.1 bitcast_select_fusion
  49.2 0.0 copy-done.1
  49.2 15.8 %shard_map.84 = f32[8,2048]{1,0:T(8,128)} custom-call(s32[64,384]{1,0:T(8,128)S(1)} %pad.12.index_ref, bf16[49,64,384]{2,1,0:T(8,128)(2,1)S(1)} %pad.13.op_ref, bf16[128,512]{1,0:T(8,128)(2,1)S(1)} %pad_maximum_fusion.1.sources_ref, f32[8,2048]{1,0:T(8,128)S(1)} %shard_map.83.near_ref, s32[64,1]{1,0:T(8,128)S(1)} %copy.13.counts_ref, ...), custom_call_target="tpu_custom_call" | custom-call | tf_op jit(solution)/shard_map/pallas_call | solution.py:266
  (7 shorter events, 0.1 us)
Async XLA Ops:
  0.0 20.8 %all-to-all-start = ((s32[8,1,8]{2,1,0:T(1,128)}), s32[8,1,8]{2,1,0:T(1,128)S(1)}, u32[]{:S(2)}, u32[]{:S(2)}) async-start(s32[8,1,8]{2,1,0:T(1,128)} %bitcast.20), calls=%async_computation | async-start | bytes 8192 | tf_op jit(solution)/shard_map/all_to_all | solution.py:227
  8.0 0.9 %copy-start = (bf16[49,2048]{1,0:T(8,128)(2,1)S(1)}, bf16[49,2048]{1,0:T(8,128)(2,1)}, u32[]{:S(2)}) copy-start(bf16[49,2048]{1,0:T(8,128)(2,1)} %harm_ref.3) | copy-start | bytes 602116
  8.9 0.8 %copy-start.2 = (bf16[1,8,2048]{2,1,0:T(8,128)(2,1)S(1)}, bf16[1,8,2048]{2,1,0:T(8,128)(2,1)}, u32[]{:S(2)}) copy-start(bf16[1,8,2048]{2,1,0:T(8,128)(2,1)} %param.8) | copy-start | bytes 98308
  10.8 17.4 %collective-permute-start.1 = (f32[16,512]{1,0:T(8,128)S(1)}, f32[16,512]{1,0:T(8,128)S(1)}, u32[]{:S(2)}, u32[]{:S(2)}) collective-permute-start(f32[16,512]{1,0:T(8,128)S(1)} %get-tuple-element.10), channel_id=1, source_target_pairs={{2,0},{4,2},{6,4},{8,6},{10,8},{12,10},{14,12},{3,1},{5,3},{7,5},{... | collective-permute-start | bytes 98312 | tf_op jit(solution)/shard_map/ppermute | solution.py:238
  12.1 16.1 %collective-permute-start = (f32[16,512]{1,0:T(8,128)S(1)}, f32[16,512]{1,0:T(8,128)S(1)}, u32[]{:S(2)}, u32[]{:S(2)}) collective-permute-start(f32[16,512]{1,0:T(8,128)S(1)} %get-tuple-element.9), channel_id=1, source_target_pairs={{0,2},{2,4},{4,6},{6,8},{8,10},{10,12},{12,14},{1,3},{3,5},{5,7},{... | collective-permute-start | bytes 98312 | tf_op jit(solution)/shard_map/ppermute | solution.py:237
  20.3 7.9 %copy-start.4 = (f32[3,2048]{1,0:T(4,128)S(1)}, f32[3,2048]{1,0:T(4,128)}, u32[]{:S(2)}) copy-start(f32[3,2048]{1,0:T(4,128)} %param.9) | copy-start | bytes 73732
  20.3 8.0 %copy-start.3 = (s32[27,64]{1,0:T(8,128)S(1)}, s32[27,64]{1,0:T(8,128)}, u32[]{:S(2)}) copy-start(s32[27,64]{1,0:T(8,128)} %near_lists_ref.1) | copy-start | bytes 20740
  20.3 28.9 %copy-start.1 = (bf16[49,2048]{1,0:T(8,128)(2,1)S(1)}, bf16[49,2048]{1,0:T(8,128)(2,1)}, u32[]{:S(2)}) copy-start(bf16[49,2048]{1,0:T(8,128)(2,1)} %harm_ref.3) | copy-start | bytes 602116
  22.2 26.9 %all-to-all-start.1 = ((bf16[8,8,512]{2,1,0:T(8,128)(2,1)}), bf16[8,8,512]{2,1,0:T(8,128)(2,1)S(1)}, u32[]{:S(2)}, u32[]{:S(2)}) async-start(bf16[8,8,512]{2,1,0:T(8,128)(2,1)} %bitcast.7), calls=%async_computation.1 | async-start | bytes 131072 | tf_op jit(solution)/shard_map/all_to_all | solution.py:228

commit v3 on v2

--- a/solution.py
+++ b/solution.py
@@ -42,7 +42,7 @@
         mask = chunk_mask(counts_ref, j, slots)
         q = charges_ref[:, j * width : (j + 1) * width].astype(F32)
         spread = jnp.where(mask[None], q[:, None, :], 0.0)
-        live_ref[:, j * width : (j + 1) * width] = jnp.sum(spread, axis=1)
+        live_ref[0:channels, j * width : (j + 1) * width] = jnp.sum(spread, axis=1)
         m = lax.dot_general(
             spread.reshape(channels * 8, width).astype(BF16),
             harm2_ref[:, j * width : (j + 1) * width],
@@ -60,17 +60,17 @@
     for b in range(window.shape[1] // 128):
         block = window[:, 128 * b : 128 * b + 128]
         for r in range(4):
-            rolled_ref[r, first_block + b] = block if r == 0 else pltpu.roll(block, 32 * r, 1)
+            rolled_ref[4 * (first_block + b) + r] = block if r == 0 else pltpu.roll(block, 32 * r, 1)
 
 
 def compute_near(near_ref, rolled_ref, pos_ref, out_ref, leaves, slots, neighbours):
     groups = -(-neighbours // 4)
-    last = rolled_ref.shape[1] - 1
+    last = rolled_ref.shape[0] - 1
     lane = lane_iota((16, 128))
 
     def body(g, carry):
         columns = pl.ds(pl.multiple_of(g * 128, 128), 128)
-        targets = jnp.transpose(pos_ref[:, columns])
+        targets = jnp.transpose(pos_ref[8:16, columns])
         kernels, charges = [], []
         for leaf in range(4):
             tgt = targets[32 * leaf : 32 * leaf + 32]
@@ -81,10 +81,9 @@
                 for j in range(4):
                     n = 4 * n4 + j
                     if n < neighbours:
-                        e = near_ref[n, g * 4 + leaf]
-                        piece = rolled_ref[(j + 4 - e % 4) % 4, e // 4]
+                        piece = rolled_ref[near_ref[n, g * 4 + leaf]]
                     else:
-                        piece = rolled_ref[0, last]
+                        piece = rolled_ref[last]
                     src = piece if src is None else jnp.where(lane >= 32 * j, piece, src)
                 squared = None
                 for k in range(3):
@@ -163,18 +162,109 @@
         out_ref[:, columns] = far + (NEAR_GAIN * alive) * near_ref[:, columns]
 
 
-def moments_kernel(dims, charges_ref, counts_ref, harm_ref, mom_ref, live_ref, harm2_ref, scratch):
-    leaves, slots = dims
+def exchange_kernel(
+    dims, near_index_ref, charges_ref, counts_ref, harm_ref, requests_ref, positions_ref,
+    sources_ref, near_ref, harm2_ref, stacked_ref, moments_ref, rolled_ref, wanted_ref, asked_ref,
+    reply_ref, got_ref, halo_ref, halo_send, halo_recv, ask_send, ask_recv, reply_send, reply_recv,
+):
+    leaves, slots, channels, neighbours, count, subs = dims
+    capacity = requests_ref.shape[0]
+    atoms = leaves * slots
+    width = HALO * slots
+    me = lax.axis_index("leaf") * subs + lax.axis_index("sub")
+
+    def device(rank):
+        return (lax.axis_index("groups"), rank // subs, rank % subs, lax.axis_index("chan"))
+
+    def peer(offset):
+        return (me + offset) % count
+
+    barrier = pltpu.get_barrier_semaphore()
+    for d in range(1, count):
+        pl.semaphore_signal(
+            barrier, inc=1, device_id=device(peer(d)), device_id_type=pl.DeviceIdType.MESH
+        )
+
+    for p in range(count):
+        wanted_ref[p] = jnp.broadcast_to(requests_ref[:, p : p + 1], (capacity, 128))
     fill_harmonics(harm_ref, harm2_ref)
-    compute_moments(charges_ref, counts_ref, harm2_ref, live_ref, scratch, leaves, slots)
-    mom_ref[...] = scratch[...].astype(BF16)
-
-
-def near_kernel(dims, near_lists_ref, window_ref, pos_ref, near_ref, rolled_ref):
-    leaves, slots, channels, neighbours = dims
-    rolled_ref[:, rolled_ref.shape[1] - 1] = jnp.zeros((4, 16, 128), F32)
-    build_rolled(window_ref[...], rolled_ref, 0)
-    compute_near(near_lists_ref, rolled_ref, pos_ref, near_ref, leaves, slots, neighbours)
+    stacked_ref[8:16, :] = jnp.zeros((8, atoms), F32)
+    stacked_ref[8:11, :] = positions_ref[...]
+    compute_moments(
+        charges_ref, counts_ref, harm2_ref, stacked_ref, moments_ref, leaves, slots
+    )
+    pl.semaphore_wait(barrier, count - 1)
+
+    def remote(src, dst, send, recv, rank):
+        return pltpu.make_async_remote_copy(
+            src_ref=src, dst_ref=dst, send_sem=send, recv_sem=recv, device_id=device(rank),
+            device_id_type=pl.DeviceIdType.MESH,
+        )
+
+    asks = []
+    for d in range(1, count):
+        copy = remote(
+            wanted_ref.at[peer(d)], asked_ref.at[d - 1], ask_send.at[d - 1], ask_recv.at[d - 1],
+            peer(d),
+        )
+        copy.start()
+        asks.append(copy)
+    halos = [
+        remote(
+            stacked_ref.at[:, pl.ds(atoms - width, width)], halo_ref.at[0], halo_send.at[0],
+            halo_recv.at[0], peer(1),
+        ),
+        remote(
+            stacked_ref.at[:, pl.ds(0, width)], halo_ref.at[1], halo_send.at[1], halo_recv.at[1],
+            peer(count - 1),
+        ),
+    ]
+    for copy in halos:
+        copy.start()
+
+    moments = moments_ref[...].astype(BF16)
+    build_rolled(stacked_ref[...], rolled_ref, width // 128)
+    for r in range(4):
+        rolled_ref[rolled_ref.shape[0] - 4 + r] = jnp.zeros((16, 128), F32)
+
+    lane = lane_iota((capacity, leaves))
+    for copy in asks:
+        copy.wait_recv()
+    hot = jnp.concatenate(
+        [jnp.where(asked_ref[d - 1][:, :leaves] == lane, 1.0, 0.0) for d in range(1, count)],
+        axis=0,
+    ).astype(BF16)
+    picked = jnp.dot(hot, moments, preferred_element_type=F32)
+    half = channels * HALF // 2
+    replies = []
+    for d in range(1, count):
+        block = picked[capacity * (d - 1) : capacity * d]
+        reply_ref[d - 1] = jnp.concatenate([block[:, :half], block[:, half:]], axis=0).astype(BF16)
+        copy = remote(
+            reply_ref.at[d - 1], got_ref.at[d - 1], reply_send.at[d - 1], reply_recv.at[d - 1],
+            peer(count - d),
+        )
+        copy.start()
+        replies.append(copy)
+
+    for copy in halos:
+        copy.wait_recv()
+    build_rolled(jnp.where(me == 0, 0.0, halo_ref[0]), rolled_ref, 0)
+    build_rolled(
+        jnp.where(me == count - 1, 0.0, halo_ref[1]), rolled_ref, (width + atoms) // 128
+    )
+    compute_near(near_index_ref, rolled_ref, stacked_ref, near_ref, leaves, slots, neighbours)
+
+    sources_ref[0:leaves, :] = moments.astype(F32)
+    sources_ref[leaves:, :] = jnp.zeros((sources_ref.shape[0] - leaves, channels * HALF), F32)
+    for d in range(1, count):
+        replies[d - 1].wait_recv()
+        block = got_ref[d - 1].astype(F32)
+        rows = pl.ds(pl.multiple_of(leaves + capacity * peer(d), 8), capacity)
+        sources_ref[rows, 0:half] = block[0:capacity]
+        sources_ref[rows, half : 2 * half] = block[capacity : 2 * capacity]
+    for copy in asks + halos + replies:
+        copy.wait_send()
 
 
 def far_kernel(
@@ -184,7 +274,7 @@
     leaves, slots, channels = dims
     fill_harmonics(harm_ref, harm2_ref)
     for b in range(table_ref.shape[0]):
-        block = sources_ref[128 * b : 128 * b + 128, :].astype(F32)
+        block = sources_ref[128 * b : 128 * b + 128, :]
         for p in range(block.shape[1] // 128):
             table_ref[b, 128 * p : 128 * p + 128, :] = jnp.transpose(
                 block[:, 128 * p : 128 * p + 128]
@@ -210,59 +300,55 @@
     vmem = pl.BlockSpec(memory_space=pltpu.VMEM)
     smem = pl.BlockSpec(memory_space=pltpu.SMEM)
     params = pltpu.CompilerParams(vmem_limit_bytes=48 * 1024 * 1024)
-
-    moments, live = pl.pallas_call(
-        functools.partial(moments_kernel, (leaves, slots)),
+    axes = ("leaf", "sub")
+    count = requests.shape[1]
+    capacity = requests.shape[2]
+    window_blocks = (leaves + 2 * HALO) * slots // 128
+    width = HALO * slots
+    peers = max(count - 1, 1)
+    turn = (jnp.arange(neighbours, dtype=jnp.int32)[:, None] - near_lists) & 3
+    near_index = (near_lists & ~3) + turn
+    dma = pltpu.SemaphoreType.DMA
+    sources, near = pl.pallas_call(
+        functools.partial(
+            exchange_kernel,
+            (leaves, slots, channels, neighbours, count, lax.axis_size("sub")),
+        ),
         out_shape=(
-            jax.ShapeDtypeStruct((leaves, channels * HALF), BF16),
+            jax.ShapeDtypeStruct((slots_pad, channels * HALF), F32),
             jax.ShapeDtypeStruct((channels, atoms), F32),
         ),
-        in_specs=[vmem] * 3,
+        in_specs=[smem] + [vmem] * 5,
         out_specs=(vmem, vmem),
-        scratch_shapes=[pltpu.VMEM((128, atoms), BF16), pltpu.VMEM((leaves, channels * HALF), F32)],
-        compiler_params=params,
-    )(charges[0], counts, harmonics)
-
-    axes = ("leaf", "sub")
-    asked = lax.all_to_all(requests[0], axes, split_axis=0, concat_axis=0, tiled=True)
-    got = lax.all_to_all(moments[asked], axes, split_axis=0, concat_axis=0, tiled=True)
-    got = got.reshape(fetched, channels * HALF)
-    stacked = jnp.concatenate(
-        [live, positions, jnp.zeros((16 - channels - 3, atoms), F32)], axis=0
-    )
-    count = lax.axis_size(axes)
-    forward = [(i, i + 1) for i in range(count - 1)]
-    backward = [(t, s) for s, t in forward]
-    width = HALO * slots
-    low = lax.ppermute(stacked[:, atoms - width :], axes, forward)
-    high = lax.ppermute(stacked[:, :width], axes, backward)
-    window = jnp.concatenate([low, stacked, high], axis=1)
+        scratch_shapes=[
+            pltpu.VMEM((128, atoms), BF16),
+            pltpu.VMEM((16, atoms), F32),
+            pltpu.VMEM((leaves, channels * HALF), F32),
+            pltpu.VMEM((4 * window_blocks + 4, 16, 128), F32),
+            pltpu.VMEM((count, capacity, 128), jnp.int32),
+            pltpu.VMEM((peers, capacity, 128), jnp.int32),
+            pltpu.VMEM((peers, 2 * capacity, channels * HALF // 2), BF16),
+            pltpu.VMEM((peers, 2 * capacity, channels * HALF // 2), BF16),
+            pltpu.VMEM((2, 16, width), F32),
+            dma((2,)),
+            dma((2,)),
+            dma((peers,)),
+            dma((peers,)),
+            dma((peers,)),
+            dma((peers,)),
+        ],
+        compiler_params=pltpu.CompilerParams(
+            vmem_limit_bytes=48 * 1024 * 1024, collective_id=0, has_side_effects=True
+        ),
+    )(near_index, charges[0], counts, harmonics, requests[0].T, positions)
+
     me = lax.axis_index(axes)
-    capacity = requests.shape[2]
     spare = leaves + capacity * me
     index = jnp.where(m2l_slots < leaves + fetched, m2l_slots, spare).T
     index = jnp.pad(index, ((0, 0), (0, types_pad - types)))
     ops = jnp.pad(
         operators.transpose(2, 1, 0), ((0, 0), (0, HALF - terms), (0, types_pad - types))
     )
-    own = jnp.arange(fetched)[:, None] // capacity == me
-    sources = jnp.concatenate(
-        [
-            moments,
-            jnp.where(own, 0, got),
-            jnp.zeros((slots_pad - leaves - fetched, channels * HALF), BF16),
-        ],
-        axis=0,
-    )
-    pos8 = jnp.pad(positions, ((0, 5), (0, 0)))
-    near = pl.pallas_call(
-        functools.partial(near_kernel, (leaves, slots, channels, neighbours)),
-        out_shape=jax.ShapeDtypeStruct((channels, atoms), F32),
-        in_specs=[smem] + [vmem] * 2,
-        out_specs=vmem,
-        scratch_shapes=[pltpu.VMEM((4, window.shape[1] // 128 + 1, 16, 128), F32)],
-        compiler_params=params,
-    )(near_lists, window, pos8)
     out = pl.pallas_call(
         functools.partial(far_kernel, (leaves, slots, channels)),
         out_shape=jax.ShapeDtypeStruct((channels, atoms), F32),

time: 65.6 us -> 37.8 us (0.58)
  starting transfers between devices: 19.1 us -> 0 us
  local copies, waits for them, and re-layouts: 6.97 us -> 2.82 us
  Pallas kernels: 37 us -> 33.7 us
  other arithmetic: 1.77 us -> 0.91 us
    all_to_all x2 -> x0, starting transfers between devices: 13.2 us -> none  [the longest x1 7.25 us: per_device(): lax.all_to_all(requests[0], axes, split_axis=0, concat_axis=0, tiled=True)]
    ppermute x2 -> x0, starting transfers between devices: 5.85 us -> none  [the longest x1 4.55 us: per_device(): low = lax.ppermute(stacked[:, atoms - width:], axes, forward)]
    pallas_call x2 -> x1, Pallas kernels: 21.2 us -> 17.9 us  [per_device(): pl.pallas_call(functools.partial(exchange_kernel, (leaves, slots, channel...]
    unnamed x11 -> x13, local copies, waits for them, and re-layouts: 3.59 us -> 2.22 us
    gather x1 -> x0, local copies, waits for them, and re-layouts: 1.33 us -> none  [per_device(): moments[asked]]
    pad x1 -> x0, local copies, waits for them, and re-layouts: 0.77 us -> none  [per_device(): pos8 = jnp.pad(positions, ((0, 5), (0, 0)))]
    slice x1 -> x0, other arithmetic: 0.73 us -> none  [per_device(): low = lax.ppermute(stacked[:, atoms - width:], axes, forward)]
  transfers between devices with their start and end apart: 4 -> 0, of which waited for: 0 -> 0; matrix products, arithmetic and copies ran while one was open for 11% -> 0% of each run, Pallas kernels for 33% -> 0%
where the time goes in v3:
time: 37.8 us; the launch traced here: 37.5 us
  Pallas kernels  33.7 us (89%)
  local copies, waits for them, and re-layouts  2.82 us (7%)
  other arithmetic  0.91 us (2%)
    pallas_call x1, Pallas kernels, per_device(): pl.pallas_call(functools.partial(exchange_kernel, (leaves, slots, channel...  17.9 us
    pallas_call x1, Pallas kernels, per_device(): pl.pallas_call(functools.partial(far_kernel, (leaves, slots, channels)),...  15.9 us
    unnamed x13, local copies, waits for them, and re-layouts  2.22 us
    transpose x1, other arithmetic, per_device(): index = jnp.where(m2l_slots < leaves + fetched, m2l_slots, spare).T  0.9 us

profile of v3, /device:TPU:0, one launch (start us, length us, event | category | flops | bytes accessed | tf_op | source)
XLA Modules:
  0.0 37.5 jit_solution(535826526258553504)
XLA Ops:
  0.0 0.9 %fusion = s32[64,316]{1,0:T(8,128)S(1)} fusion(s32[316,64]{0,1:T(8,128)} %param.15, s32[]{:T(128)S(6)} %add_shard_map.3), kind=kLoop, calls=%fused_computation.2 | loop fusion | flops 40448 | bytes 161796 | tf_op jit(solution)/shard_map/transpose | solution.py:347
  0.9 1.9 %copy.14 = bf16[316,49,49]{0,1,2:T(8,128)(2,1)S(1)} copy(bf16[316,49,49]{0,2,1:T(8,128)(2,1)} %param.11) | data formatting | bytes 3034864 | tf_op args[3]
  2.8 0.0 copy-start.3
  2.8 0.0 copy-start.5
  2.8 0.0 copy-start.4
  2.8 0.0 copy-start
  2.8 0.0 copy-start.1
  2.9 0.0 copy-start.2
  2.9 0.4 %pad.9.op_ref = bf16[49,64,384]{2,1,0:T(8,128)(2,1)S(1)} pad(bf16[49,49,316]{2,1,0:T(8,128)(2,1)S(1)} %bitcast.12, bf16[]{:T(256)} %constant.22.clone.1), padding=0_0x0_15x0_68 | pad | bytes 3925882 | tf_op jit(solution)/shard_map/jit(_pad)/pad | solution.py:349
  3.3 0.2 copy-done.3
  3.5 0.0 copy-done.5
  3.5 0.1 copy.11.counts_ref
  3.6 0.0 copy-done.4
  3.6 0.1 copy.10
  3.7 0.1 copy-done
  3.8 0.0 copy-done.1
  3.8 0.0 copy-done.2
  3.8 17.9 %shard_map.82 = (f32[128,512]{1,0:T(8,128)S(1)}, f32[8,2048]{1,0:T(8,128)S(1)}) custom-call(s32[27,64]{1,0:T(8,128)S(1)} %and_add_fusion.near_index_ref, bf16[8,2048]{1,0:T(8,128)(2,1)S(1)} %bitcast.10, s32[64,1]{1,0:T(8,128)S(1)} %copy.11.counts_ref, bf16[49,2048]{1,0:T(8,128)(2,1)S(1)} %copy-done, s32[8,8]{1,0:T(8,128)S(1)} %bitcast.11, ...), custom_call_target="tpu_custom_call" | custom-call | tf_op jit(solution)/shard_map/pallas_call | solution.py:312
  21.7 15.9 %shard_map.83 = f32[8,2048]{1,0:T(8,128)} custom-call(s32[64,384]{1,0:T(8,128)S(1)} %pad.8.index_ref, bf16[49,64,384]{2,1,0:T(8,128)(2,1)S(1)} %pad.9.op_ref, f32[128,512]{1,0:T(8,128)S(1)} %get-tuple-element.7.sources_ref, f32[8,2048]{1,0:T(8,128)S(1)} %get-tuple-element.8.near_ref, s32[64,1]{1,0:T(8,128)S(1)} %copy.11.counts_ref, bf16[49,2048]{1,0:T(8,128)(2,1)S(1)} %copy-done), custom_call_target="tpu_custom_call" | custom-call | tf_op jit(solution)/shard_map/pallas_call | solution.py:352
  (2 shorter events, 0.0 us)
Async XLA Ops:
  2.8 0.7 %copy-start.3 = (s32[27,64]{1,0:T(8,128)S(1)}, s32[27,64]{1,0:T(8,128)}, u32[]{:S(2)}) copy-start(s32[27,64]{1,0:T(8,128)} %param.13) | copy-start | bytes 20740
  2.8 0.7 %copy-start.5 = (s32[1,64]{1,0:T(1,128)S(1)}, s32[1,64]{1,0:T(1,128)}, u32[]{:S(2)}) copy-start(s32[1,64]{1,0:T(1,128)} %param.12) | copy-start | bytes 772
  2.8 0.8 %copy-start.4 = (s32[1,8,8]{2,1,0:T(8,128)S(1)}, s32[1,8,8]{2,1,0:T(8,128)}, u32[]{:S(2)}) copy-start(s32[1,8,8]{2,1,0:T(8,128)} %param.14) | copy-start | bytes 772
  2.8 1.0 %copy-start = (bf16[49,2048]{1,0:T(8,128)(2,1)S(1)}, bf16[49,2048]{1,0:T(8,128)(2,1)}, u32[]{:S(2)}) copy-start(bf16[49,2048]{1,0:T(8,128)(2,1)} %harm_ref.3) | copy-start | bytes 602116
  2.8 0.9 %copy-start.1 = (bf16[1,8,2048]{2,1,0:T(8,128)(2,1)S(1)}, bf16[1,8,2048]{2,1,0:T(8,128)(2,1)}, u32[]{:S(2)}) copy-start(bf16[1,8,2048]{2,1,0:T(8,128)(2,1)} %param.8) | copy-start | bytes 98308
  2.9 0.9 %copy-start.2 = (f32[3,2048]{1,0:T(4,128)S(1)}, f32[3,2048]{1,0:T(4,128)}, u32[]{:S(2)}) copy-start(f32[3,2048]{1,0:T(4,128)} %positions_ref.1) | copy-start | bytes 73732

commit v4 on v3

--- a/solution.py
+++ b/solution.py
@@ -110,39 +110,75 @@
     return jnp.take_along_axis(row, index, axis=1, mode="promise_in_bounds")
 
 
-def compute_local(index_ref, op_ref, table_ref, acc_ref, leaves, channels):
+def compute_local(index_ref, op_ref, table_ref, tail_ref, acc_ref, leaves, channels):
     terms, _, types_pad = op_ref.shape
     blocks = table_ref.shape[0]
     batch = math.gcd(terms, 7)
+    shared = tail_ref is not None
+    whole = types_pad // 128 - (1 if shared else 0)
+    low = lane_iota((8, 128)) < HALF
     acc_ref[...] = jnp.zeros_like(acc_ref)
+    if shared:
+        for pair in range(leaves // 16):
+            first = index_ref[16 * pair : 16 * pair + 8, 128 * whole :]
+            second = index_ref[16 * pair + 8 : 16 * pair + 16, 128 * whole :]
+            tail_ref[8 * pair : 8 * pair + 8, :] = jnp.where(low, first, pltpu.roll(second, HALF, 1))
+
+    def lookup(lines, index):
+        if blocks == 1:
+            return gather_lanes(lines[0], index)
+        got = jnp.zeros((8, 128), F32)
+        for b in range(blocks):
+            got = jnp.where(index // 128 == b, gather_lanes(lines[b], index % 128), got)
+        return got
 
     def body(step, carry):
-        parts = []
+        found = {}
+        lines = {}
         for k in range(batch):
-            v = step * batch + k
-            rows = []
             for c in range(channels):
-                lines = [
-                    jnp.broadcast_to(table_ref[b, pl.ds(c * HALF + v, 1), :], (8, 128))
+                lines[k, c] = [
+                    jnp.broadcast_to(
+                        table_ref[b, pl.ds(c * HALF + step * batch + k, 1), :], (8, 128)
+                    )
                     for b in range(blocks)
                 ]
-                for l8 in range(leaves // 8):
-                    columns = []
-                    for t in range(types_pad // 128):
-                        index = index_ref[8 * l8 : 8 * l8 + 8, 128 * t : 128 * t + 128]
-                        if blocks == 1:
-                            got = gather_lanes(lines[0], index)
-                        else:
-                            got = jnp.zeros((8, 128), F32)
-                            for b in range(blocks):
-                                piece = gather_lanes(lines[b], index % 128)
-                                got = jnp.where(index // 128 == b, piece, got)
-                        columns.append(got)
-                    rows.append(jnp.concatenate(columns, axis=1))
+
+        def find(k, c, l8, t):
+            if t < whole:
+                index = index_ref[8 * l8 : 8 * l8 + 8, 128 * t : 128 * t + 128]
+                found[k, c, l8, t] = lookup(lines[k, c], index)
+            elif l8 % 2 == 0:
+                got = lookup(lines[k, c], tail_ref[4 * l8 : 4 * l8 + 8, :])
+                found[k, c, l8, t] = jnp.where(low, got, 0.0)
+                found[k, c, l8 + 1, t] = jnp.where(low, 0.0, got)
+
+        for l8 in range(leaves // 8):
+            for t in range(types_pad // 128):
+                for k in range(batch):
+                    for c in range(channels):
+                        find(k, c, l8, t)
+        parts, ops = [], []
+        for k in range(batch):
+            rows = [
+                jnp.concatenate([found[k, c, l8, t] for t in range(types_pad // 128)], axis=1)
+                for c in range(channels)
+                for l8 in range(leaves // 8)
+            ]
             parts.append(jnp.concatenate(rows, axis=0).astype(BF16))
-        sources = jnp.concatenate(parts, axis=1)
-        ops = jnp.concatenate([op_ref[step * batch + k] for k in range(batch)], axis=1)
-        acc_ref[...] += lax.dot_general(sources, ops, NT, preferred_element_type=F32)
+            op = op_ref[step * batch + k]
+            if shared:
+                ops.append(op[:, : 128 * whole])
+                last = op[:, 128 * whole :].astype(F32)
+                ops.append((last + pltpu.roll(last, HALF, 1)).astype(BF16))
+            else:
+                ops.append(op)
+        acc_ref[...] += lax.dot_general(
+            jnp.concatenate(parts, axis=1),
+            jnp.concatenate(ops, axis=1),
+            NT,
+            preferred_element_type=F32,
+        )
         return carry
 
     lax.fori_loop(0, terms // batch, body, 0)
@@ -269,7 +305,7 @@
 
 def far_kernel(
     dims, index_ref, op_ref, sources_ref, near_ref, counts_ref, harm_ref, out_ref, harm2_ref,
-    table_ref, acc_ref,
+    table_ref, acc_ref, tail_ref=None,
 ):
     leaves, slots, channels = dims
     fill_harmonics(harm_ref, harm2_ref)
@@ -279,7 +315,7 @@
             table_ref[b, 128 * p : 128 * p + 128, :] = jnp.transpose(
                 block[:, 128 * p : 128 * p + 128]
             )
-    compute_local(index_ref, op_ref, table_ref, acc_ref, leaves, channels)
+    compute_local(index_ref, op_ref, table_ref, tail_ref, acc_ref, leaves, channels)
     finish(acc_ref, harm2_ref, counts_ref, near_ref, out_ref, leaves, slots, channels)
 
 
@@ -358,7 +394,8 @@
             pltpu.VMEM((128, atoms), BF16),
             pltpu.VMEM((slots_pad // 128, channels * HALF, 128), F32),
             pltpu.VMEM((channels * leaves, HALF), F32),
-        ],
+        ]
+        + ([pltpu.VMEM((leaves // 2, 128), jnp.int32)] if 0 < types % 128 <= HALF else []),
         compiler_params=params,
     )(index, ops, sources, near, counts, harmonics)
     return out[None]

time: 37.8 us -> 32.6 us (0.86)
  Pallas kernels: 33.7 us -> 28.6 us
    pallas_call x1, Pallas kernels: 15.9 us -> 10.7 us  [per_device(): pl.pallas_call(functools.partial(far_kernel, (leaves, slots, channels)),...]
where the time goes in v4:
time: 32.6 us; the launch traced here: 32.4 us
  Pallas kernels  28.6 us (88%)
  local copies, waits for them, and re-layouts  2.82 us (9%)
  other arithmetic  0.91 us (3%)
    pallas_call x1, Pallas kernels, per_device(): pl.pallas_call(functools.partial(exchange_kernel, (leaves, slots, channel...  17.9 us
    pallas_call x1, Pallas kernels, per_device(): pl.pallas_call(functools.partial(far_kernel, (leaves, slots, channels)),...  10.7 us
    unnamed x13, local copies, waits for them, and re-layouts  2.22 us
    transpose x1, other arithmetic, per_device(): index = jnp.where(m2l_slots < leaves + fetched, m2l_slots, spare).T  0.9 us

profile of v4, /device:TPU:0, one launch (start us, length us, event | category | flops | bytes accessed | tf_op | source)
XLA Modules:
  0.0 32.4 jit_solution(2496877609241819713)
XLA Ops:
  0.0 0.9 %fusion = s32[64,316]{1,0:T(8,128)S(1)} fusion(s32[316,64]{0,1:T(8,128)} %param.15, s32[]{:T(128)S(6)} %add_shard_map.3), kind=kLoop, calls=%fused_computation.2 | loop fusion | flops 40448 | bytes 161796 | tf_op jit(solution)/shard_map/transpose | solution.py:383
  0.9 1.9 %copy.14 = bf16[316,49,49]{0,1,2:T(8,128)(2,1)S(1)} copy(bf16[316,49,49]{0,2,1:T(8,128)(2,1)} %param.11) | data formatting | bytes 3034864 | tf_op args[3]
  2.8 0.0 copy-start.3
  2.8 0.0 copy-start.5
  2.8 0.0 copy-start.4
  2.8 0.0 copy-start
  2.8 0.0 copy-start.1
  2.9 0.0 copy-start.2
  2.9 0.4 %pad.9.op_ref = bf16[49,64,384]{2,1,0:T(8,128)(2,1)S(1)} pad(bf16[49,49,316]{2,1,0:T(8,128)(2,1)S(1)} %bitcast.12, bf16[]{:T(256)} %constant.22.clone.1), padding=0_0x0_15x0_68 | pad | bytes 3925882 | tf_op jit(solution)/shard_map/jit(_pad)/pad | solution.py:385
  3.3 0.2 copy-done.3
  3.5 0.0 copy-done.5
  3.5 0.1 copy.11.counts_ref
  3.6 0.0 copy-done.4
  3.6 0.1 copy.10
  3.7 0.1 copy-done
  3.8 0.0 copy-done.1
  3.8 0.0 copy-done.2
  3.8 17.9 %shard_map.82 = (f32[128,512]{1,0:T(8,128)S(1)}, f32[8,2048]{1,0:T(8,128)S(1)}) custom-call(s32[27,64]{1,0:T(8,128)S(1)} %and_add_fusion.near_index_ref, bf16[8,2048]{1,0:T(8,128)(2,1)S(1)} %bitcast.10, s32[64,1]{1,0:T(8,128)S(1)} %copy.11.counts_ref, bf16[49,2048]{1,0:T(8,128)(2,1)S(1)} %copy-done, s32[8,8]{1,0:T(8,128)S(1)} %bitcast.11, ...), custom_call_target="tpu_custom_call" | custom-call | tf_op jit(solution)/shard_map/pallas_call | solution.py:348
  21.7 10.7 %shard_map.83 = f32[8,2048]{1,0:T(8,128)} custom-call(s32[64,384]{1,0:T(8,128)S(1)} %pad.8.index_ref, bf16[49,64,384]{2,1,0:T(8,128)(2,1)S(1)} %pad.9.op_ref, f32[128,512]{1,0:T(8,128)S(1)} %get-tuple-element.7.sources_ref, f32[8,2048]{1,0:T(8,128)S(1)} %get-tuple-element.8.near_ref, s32[64,1]{1,0:T(8,128)S(1)} %copy.11.counts_ref, bf16[49,2048]{1,0:T(8,128)(2,1)S(1)} %copy-done), custom_call_target="tpu_custom_call" | custom-call | tf_op jit(solution)/shard_map/pallas_call | solution.py:388
  (2 shorter events, 0.0 us)
Async XLA Ops:
  2.8 0.7 %copy-start.3 = (s32[27,64]{1,0:T(8,128)S(1)}, s32[27,64]{1,0:T(8,128)}, u32[]{:S(2)}) copy-start(s32[27,64]{1,0:T(8,128)} %param.13) | copy-start | bytes 20740
  2.8 0.7 %copy-start.5 = (s32[1,64]{1,0:T(1,128)S(1)}, s32[1,64]{1,0:T(1,128)}, u32[]{:S(2)}) copy-start(s32[1,64]{1,0:T(1,128)} %param.12) | copy-start | bytes 772
  2.8 0.8 %copy-start.4 = (s32[1,8,8]{2,1,0:T(8,128)S(1)}, s32[1,8,8]{2,1,0:T(8,128)}, u32[]{:S(2)}) copy-start(s32[1,8,8]{2,1,0:T(8,128)} %param.14) | copy-start | bytes 772
  2.8 1.0 %copy-start = (bf16[49,2048]{1,0:T(8,128)(2,1)S(1)}, bf16[49,2048]{1,0:T(8,128)(2,1)}, u32[]{:S(2)}) copy-start(bf16[49,2048]{1,0:T(8,128)(2,1)} %harm_ref.3) | copy-start | bytes 602116
  2.8 0.9 %copy-start.1 = (bf16[1,8,2048]{2,1,0:T(8,128)(2,1)S(1)}, bf16[1,8,2048]{2,1,0:T(8,128)(2,1)}, u32[]{:S(2)}) copy-start(bf16[1,8,2048]{2,1,0:T(8,128)(2,1)} %param.8) | copy-start | bytes 98308
  2.9 0.9 %copy-start.2 = (f32[3,2048]{1,0:T(4,128)S(1)}, f32[3,2048]{1,0:T(4,128)}, u32[]{:S(2)}) copy-start(f32[3,2048]{1,0:T(4,128)} %positions_ref.1) | copy-start | bytes 73732

commit v5 on v4

--- a/solution.py
+++ b/solution.py
@@ -103,7 +103,7 @@
         out_ref[:, columns] = near
         return carry
 
-    lax.fori_loop(0, leaves // 4, body, 0)
+    lax.fori_loop(0, leaves // 4, body, 0, unroll=2)
 
 
 def gather_lanes(row, index):

time: 32.6 us -> 31.5 us (0.966)
  Pallas kernels: 28.6 us -> 27.4 us
    pallas_call x1, Pallas kernels: 17.9 us -> 16.7 us  [per_device(): pl.pallas_call(functools.partial(exchange_kernel, (leaves, slots, channel...]
where the time goes in v5:
time: 31.5 us; the launch traced here: 31.2 us
  Pallas kernels  27.4 us (87%)
  local copies, waits for them, and re-layouts  2.82 us (9%)
  other arithmetic  0.91 us (3%)
    pallas_call x1, Pallas kernels, per_device(): pl.pallas_call(functools.partial(exchange_kernel, (leaves, slots, channel...  16.7 us
    pallas_call x1, Pallas kernels, per_device(): pl.pallas_call(functools.partial(far_kernel, (leaves, slots, channels)),...  10.7 us
    unnamed x13, local copies, waits for them, and re-layouts  2.22 us
    transpose x1, other arithmetic, per_device(): index = jnp.where(m2l_slots < leaves + fetched, m2l_slots, spare).T  0.9 us

profile of v5, /device:TPU:0, one launch (start us, length us, event | category | flops | bytes accessed | tf_op | source)
XLA Modules:
  0.0 31.2 jit_solution(11162844133958314870)
XLA Ops:
  0.0 0.9 %fusion = s32[64,316]{1,0:T(8,128)S(1)} fusion(s32[316,64]{0,1:T(8,128)} %param.15, s32[]{:T(128)S(6)} %add_shard_map.3), kind=kLoop, calls=%fused_computation.2 | loop fusion | flops 40448 | bytes 161796 | tf_op jit(solution)/shard_map/transpose | solution.py:383
  0.9 1.9 %copy.14 = bf16[316,49,49]{0,1,2:T(8,128)(2,1)S(1)} copy(bf16[316,49,49]{0,2,1:T(8,128)(2,1)} %param.11) | data formatting | bytes 3034864 | tf_op args[3]
  2.8 0.0 copy-start.3
  2.8 0.0 copy-start.5
  2.8 0.0 copy-start.4
  2.8 0.0 copy-start
  2.8 0.0 copy-start.1
  2.9 0.0 copy-start.2
  2.9 0.4 %pad.9.op_ref = bf16[49,64,384]{2,1,0:T(8,128)(2,1)S(1)} pad(bf16[49,49,316]{2,1,0:T(8,128)(2,1)S(1)} %bitcast.12, bf16[]{:T(256)} %constant.22.clone.1), padding=0_0x0_15x0_68 | pad | bytes 3925882 | tf_op jit(solution)/shard_map/jit(_pad)/pad | solution.py:385
  3.3 0.2 copy-done.3
  3.5 0.0 copy-done.5
  3.5 0.1 copy.11.counts_ref
  3.6 0.0 copy-done.4
  3.6 0.1 copy.10
  3.7 0.1 copy-done
  3.8 0.0 copy-done.1
  3.8 0.0 copy-done.2
  3.8 16.7 %shard_map.82 = (f32[128,512]{1,0:T(8,128)S(1)}, f32[8,2048]{1,0:T(8,128)S(1)}) custom-call(s32[27,64]{1,0:T(8,128)S(1)} %and_add_fusion.near_index_ref, bf16[8,2048]{1,0:T(8,128)(2,1)S(1)} %bitcast.10, s32[64,1]{1,0:T(8,128)S(1)} %copy.11.counts_ref, bf16[49,2048]{1,0:T(8,128)(2,1)S(1)} %copy-done, s32[8,8]{1,0:T(8,128)S(1)} %bitcast.11, ...), custom_call_target="tpu_custom_call" | custom-call | tf_op jit(solution)/shard_map/pallas_call | solution.py:348
  20.5 10.7 %shard_map.83 = f32[8,2048]{1,0:T(8,128)} custom-call(s32[64,384]{1,0:T(8,128)S(1)} %pad.8.index_ref, bf16[49,64,384]{2,1,0:T(8,128)(2,1)S(1)} %pad.9.op_ref, f32[128,512]{1,0:T(8,128)S(1)} %get-tuple-element.7.sources_ref, f32[8,2048]{1,0:T(8,128)S(1)} %get-tuple-element.8.near_ref, s32[64,1]{1,0:T(8,128)S(1)} %copy.11.counts_ref, bf16[49,2048]{1,0:T(8,128)(2,1)S(1)} %copy-done), custom_call_target="tpu_custom_call" | custom-call | tf_op jit(solution)/shard_map/pallas_call | solution.py:388
  (2 shorter events, 0.0 us)
Async XLA Ops:
  2.8 0.7 %copy-start.3 = (s32[27,64]{1,0:T(8,128)S(1)}, s32[27,64]{1,0:T(8,128)}, u32[]{:S(2)}) copy-start(s32[27,64]{1,0:T(8,128)} %param.13) | copy-start | bytes 20740
  2.8 0.7 %copy-start.5 = (s32[1,64]{1,0:T(1,128)S(1)}, s32[1,64]{1,0:T(1,128)}, u32[]{:S(2)}) copy-start(s32[1,64]{1,0:T(1,128)} %param.12) | copy-start | bytes 772
  2.8 0.8 %copy-start.4 = (s32[1,8,8]{2,1,0:T(8,128)S(1)}, s32[1,8,8]{2,1,0:T(8,128)}, u32[]{:S(2)}) copy-start(s32[1,8,8]{2,1,0:T(8,128)} %param.14) | copy-start | bytes 772
  2.8 1.0 %copy-start = (bf16[49,2048]{1,0:T(8,128)(2,1)S(1)}, bf16[49,2048]{1,0:T(8,128)(2,1)}, u32[]{:S(2)}) copy-start(bf16[49,2048]{1,0:T(8,128)(2,1)} %harm_ref.3) | copy-start | bytes 602116
  2.8 0.9 %copy-start.1 = (bf16[1,8,2048]{2,1,0:T(8,128)(2,1)S(1)}, bf16[1,8,2048]{2,1,0:T(8,128)(2,1)}, u32[]{:S(2)}) copy-start(bf16[1,8,2048]{2,1,0:T(8,128)(2,1)} %param.8) | copy-start | bytes 98308
  2.9 0.9 %copy-start.2 = (f32[3,2048]{1,0:T(4,128)S(1)}, f32[3,2048]{1,0:T(4,128)}, u32[]{:S(2)}) copy-start(f32[3,2048]{1,0:T(4,128)} %positions_ref.1) | copy-start | bytes 73732
